TPU v7x, 512 devices: a whole 4x4x16 slice. The times are simulated.
512 devices in a mesh: grp: 16 (over y, z_lo), dev: 32 (over z_hi, x, core).
Axes of the slice: x: 4, y: 4, z: 16 (z_hi: 4, z_lo: 4; z = z_hi * 4 + z_lo), core: 2. Of those that a mesh axis runs over, the one named last changes fastest.
Arguments:
- lhs_table: bfloat16 [65536, 400], P(('grp', 'dev')), may hold values from -0.29882812 to 0.29882812
- lhs_state: float32 [65536], P(('grp', 'dev')), may hold values from 0.01 to 1
- rhs_table: bfloat16 [65536, 400], P(('grp', 'dev')), may hold values from -0.29882812 to 0.29882812
- rhs_state: float32 [65536], P(('grp', 'dev')), may hold values from 0.01 to 1
- relations: float32 [2080, 400], P('dev'), may hold values from -1.8 to 1.8
- rel_state: float32 [2080], P('dev'), may hold values from 1e-05 to 0.1
- src_index: int32 [512, 2, 512], P(('grp', 'dev')), may hold values from 0 to 127
- dst_index: int32 [512, 2, 512], P(('grp', 'dev')), may hold values from 0 to 127
- rel_index: int32 [512, 2, 512], P(('grp', 'dev')), may hold values from 0 to 2079
- neg_index: int32 [512, 2, 512], P(('grp', 'dev')), may hold values from 0 to 127
- edge_count: int32 [512, 2], P(('grp', 'dev')), may hold values from 128 to 512, as said below
Outputs:
- lhs_out: bfloat16 [65536, 400], P(('grp', 'dev'))
- lhs_state_out: float32 [65536], P(('grp', 'dev'))
- rhs_out: bfloat16 [65536, 400], P(('grp', 'dev'))
- rhs_state_out: float32 [65536], P(('grp', 'dev'))
- relations_out: float32 [2080, 400], P('dev')
- rel_state_out: float32 [2080], P('dev')
Inputs may be any that keep to these rules, and one draw needn't show every extreme that they name: Edges of a bucket are live in its first edge_count slots; at least a quarter of the slots are live and some bucket is full.
All inputs are finite; a program needn't handle non-finite values.
Results may differ from a plain program's by a relative error of at most 0.001.
The roundings to bfloat16 on the way count: a program that leaves them out, or rounds other values in their place, can miss the bound.
Values may be sent and summed in bfloat16 or wider, within the bound.
A program may use at most 64 MiB of HBM per device.

v0:
```python
import jax
import jax.numpy as jnp
from jax import lax
from jax.sharding import PartitionSpec as P

LEARN = 0.1
EPSILON = 1e-06


def from_behind(value, axis, steps):
    count = lax.axis_size(axis)
    pairs = [(source, (source + steps) % count) for source in range(count)]
    return lax.ppermute(value, axis, pairs)


def row_adagrad(rows, state, grad):
    new_state = state + jnp.mean(grad * grad, axis=-1)
    moved = rows.astype(jnp.float32) - LEARN * grad / (jnp.sqrt(new_state) + EPSILON)[:, None]
    return (moved.astype(jnp.bfloat16), new_state)


def one_hot(index, count):
    return (index[:, None] == jnp.arange(count, dtype=jnp.int32)[None, :]).astype(jnp.bfloat16)


def spread_rows(hot, grad):
    return lax.dot_general(
        hot.astype(jnp.float32),
        grad,
        (((0,), (0,)), ((), ())),
        precision=lax.Precision.HIGHEST,
        preferred_element_type=jnp.float32,
    )


def train_round(lhs, lhs_st, rhs, rhs_st, table, source, target, kinds, negatives, count):
    parts_rows = lhs.shape[0]
    width = lhs.shape[1]
    half = width // 2
    slots = source.shape[0]
    live = (jnp.arange(slots, dtype=jnp.int32) < count).astype(jnp.float32)
    src_hot = one_hot(source, parts_rows)
    dst_hot = one_hot(target, parts_rows)
    neg_hot = one_hot(negatives, parts_rows)
    left = jnp.dot(src_hot, lhs, preferred_element_type=jnp.float32)
    right_wide = jnp.dot(dst_hot, rhs, preferred_element_type=jnp.float32)
    noise = jnp.dot(neg_hot, rhs, preferred_element_type=jnp.float32).astype(jnp.bfloat16)
    oper = table[kinds].astype(jnp.float32)
    a_re, a_im = (left[:, :half], left[:, half:])
    r_re, r_im = (oper[:, :half], oper[:, half:])
    query = jnp.concatenate([a_re * r_re - a_im * r_im, a_re * r_im + a_im * r_re], axis=1)
    q_bf = query.astype(jnp.bfloat16)
    q_wide = q_bf.astype(jnp.float32)
    pos = jnp.sum(q_wide * right_wide, axis=1)
    neg = lax.dot_general(q_bf, noise, (((1,), (1,)), ((), ())), preferred_element_type=jnp.float32)
    pos_exp = jnp.exp(pos)
    neg_exp = jnp.exp(neg)
    total = pos_exp + jnp.sum(neg_exp, axis=1)
    w_pos = live * (pos_exp / total - 1.0)
    w_neg = (live[:, None] * neg_exp / total[:, None]).astype(jnp.bfloat16)
    dq = w_pos[:, None] * right_wide + jnp.dot(w_neg, noise, preferred_element_type=jnp.float32)
    grad_y = w_pos[:, None] * q_wide
    grad_n = lax.dot_general(
        w_neg, q_bf, (((0,), (0,)), ((), ())), preferred_element_type=jnp.float32
    )
    dq_re, dq_im = (dq[:, :half], dq[:, half:])
    grad_a = jnp.concatenate([dq_re * r_re + dq_im * r_im, dq_im * r_re - dq_re * r_im], axis=1)
    grad_r = jnp.concatenate([dq_re * a_re + dq_im * a_im, dq_im * a_re - dq_re * a_im], axis=1)
    lhs_grad = spread_rows(src_hot, grad_a)
    rhs_grad = spread_rows(dst_hot, grad_y) + spread_rows(neg_hot, grad_n)
    rel_grad = jax.ops.segment_sum(grad_r, kinds, table.shape[0])
    lhs_new, lhs_st_new = row_adagrad(lhs, lhs_st, lhs_grad)
    rhs_new, rhs_st_new = row_adagrad(rhs, rhs_st, rhs_grad)
    return (lhs_new, lhs_st_new, rhs_new, rhs_st_new, rel_grad)


def body(
    lhs_table,
    lhs_state,
    rhs_table,
    rhs_state,
    relations,
    rel_state,
    src_index,
    dst_index,
    rel_index,
    neg_index,
    edge_count,
):
    table = lax.all_gather(relations.astype(jnp.bfloat16), "dev", axis=0, tiled=True)
    lhs, lhs_st, rhs, rhs_st = (lhs_table, lhs_state, rhs_table, rhs_state)
    accum = jnp.zeros(table.shape, jnp.float32)
    for turn in range(src_index.shape[1]):
        if turn > 0:
            rhs, rhs_st = (
                from_behind(rhs.astype(jnp.float32), "dev", 1).astype(rhs.dtype),
                from_behind(rhs_st, "dev", 1),
            )
        lhs, lhs_st, rhs, rhs_st, grads = train_round(
            lhs,
            lhs_st,
            rhs,
            rhs_st,
            table,
            src_index[0, turn],
            dst_index[0, turn],
            rel_index[0, turn],
            neg_index[0, turn],
            edge_count[0, turn],
        )
        accum = accum + grads
    shard_rows = relations.shape[0]
    whole = lax.psum(accum, ("grp", "dev"))
    mine = lax.dynamic_slice_in_dim(whole, lax.axis_index("dev") * shard_rows, shard_rows, 0)
    new_rel_state = rel_state + jnp.mean(mine * mine, axis=1)
    new_relations = relations - LEARN * mine / (jnp.sqrt(new_rel_state) + EPSILON)[:, None]
    return (lhs, lhs_st, rhs, rhs_st, new_relations, new_rel_state)


def solution(mesh):
    return jax.shard_map(
        body,
        mesh=mesh,
        in_specs=(
            P(("grp", "dev"), None),
            P(("grp", "dev")),
            P(("grp", "dev"), None),
            P(("grp", "dev")),
            P("dev", None),
            P("dev"),
            P(("grp", "dev"), None, None),
            P(("grp", "dev"), None, None),
            P(("grp", "dev"), None, None),
            P(("grp", "dev"), None, None),
            P(("grp", "dev"), None),
        ),
        out_specs=(
            P(("grp", "dev"), None),
            P(("grp", "dev")),
            P(("grp", "dev"), None),
            P(("grp", "dev")),
            P("dev", None),
            P("dev"),
        ),
        check_vma=False,
    )
```

profile of v0, /device:TPU:1, one launch (start us, length us, event | category | flops | bytes accessed | tf_op | source)
XLA Modules:
  0.0 630.7 jit_solution(12121976338034221701)
XLA Ops:
  7.2 0.0 all-gather.3.cloned.1.call-start
  7.2 1.6 convert_bitcast_fusion
  8.8 0.0 all-gather.3.cloned.1.call-update
  8.8 0.0 all-reduce.2.cloned.1.call-start
  8.8 1.3 fusion.45
  10.2 0.6 fusion.34
  10.8 0.7 fusion.33
  11.5 0.8 compare_select_fusion
  12.3 0.8 slice_bitcast_fusion.1
  13.0 0.8 fusion.42
  13.8 0.8 fusion.43
  14.6 0.8 fusion.44
  15.3 2.0 convolution_convert_fusion.1
  17.4 2.2 fusion.19
  19.5 78.3 %all-gather.3.cloned.1.call-done = bf16[32,65,400]{2,1,0:T(8,128)(2,1)} async-done(((bf16[1,65,400]{2,1,0:T(8,128)(2,1)}), bf16[32,65,400]{2,1,0:T(8,128)(2,1)}) %all-gather.3.cloned.1.call-update) | async-done | bytes 1664016 | tf_op jit(solution)/shard_map/all_gather | solution.py:90
  97.8 2.9 reshape.144
  100.7 2.0 gather_fusion.1
  102.7 0.2 copy.23
  102.9 0.1 convert_element_type.94
  103.0 2.0 gather_fusion
  105.0 0.0 copy-start.1
  105.0 0.2 copy.22
  105.2 0.1 convert_element_type.87
  105.3 0.8 copy-done
  106.1 0.2 subtract_convert_fusion.1
  106.4 0.4 fusion.2
  106.8 0.5 fusion.46
  107.3 0.7 exponential_add_fusion.1
  107.9 0.6 fusion.3
  108.6 0.4 fusion.40
  109.0 0.4 convolution_add_fusion
  109.4 0.0 copy-start.6
  109.4 0.3 multiply_add_fusion.2
  109.7 0.0 copy-start.5
  109.7 0.0 copy-start.3
  109.7 0.6 multiply_reduce_fusion.2
  110.4 3.5 collective-permute-start
  113.9 2.4 collective-permute-start.1
  116.3 0.6 multiply_reduce_fusion.3
  117.0 0.4 fusion.17
  117.3 0.2 subtract_convert_fusion
  117.6 0.4 convolution_convert_fusion
  118.0 0.5 fusion.47
  118.5 0.4 fusion.4
  118.9 0.7 exponential_add_fusion
  119.5 0.6 fusion.5
  120.2 0.4 multiply_add_fusion
  120.6 0.3 multiply_add_fusion.1
  120.9 0.1 maximum_maximum_fusion
  121.0 1.8 copy.24
  122.8 9.4 %scatter_custom_fusion = f32[2080,400]{1,0:T(8,128)} fusion(s32[1024]{0:T(1024)S(1)} %bitcast.47, f32[1024,400]{1,0:T(8,128)} %copy.24, f32[]{:T(128)} %constant.12.clone.1), kind=kCustom, calls=%fused_computation.3 | custom fusion | flops 409600 | bytes 3328512 | tf_op jit(solution)/shard_map/add | solution.py:111
  132.3 0.0 all-reduce.2.cloned.1.call-update
  132.3 1.2 copy-done.9
  133.5 0.4 fusion.39
  133.9 0.6 multiply_reduce_fusion
  134.6 0.5 sqrt_add_fusion.1
  135.1 0.6 multiply_reduce_fusion.1
  135.7 0.5 sqrt_add_fusion.2
  136.2 0.7 subtract_convert_fusion.3
  136.9 0.7 subtract_convert_fusion.2
  137.6 483.0 %all-reduce.2.cloned.1.call-done = f32[2080,400]{1,0:T(8,128)} async-done(((f32[2080,400]{1,0:T(8,128)}), f32[2080,400]{1,0:T(8,128)}) %all-reduce.2.cloned.1.call-update) | async-done | bytes 3328016 | tf_op jit(solution)/shard_map/psum | solution.py:113
  620.6 1.0 multiply_reduce_fusion.4
  621.6 0.5 sqrt_add_fusion
  622.2 1.7 divide_subtract_fusion
  (23 shorter events, 0.2 us)
Async XLA Ops:
  7.2 90.7 %all-gather.3.cloned.1.call-start = ((), (), s32[]{:S(2)}) async-start(), calls=%async_computation.1 | async-start | bytes 2433024 | tf_op jit(solution)/shard_map/all_gather | solution.py:90
  8.8 611.8 %all-reduce.2.cloned.1.call-start = ((), (), s32[]{:S(2)}) async-start(), calls=%async_computation | async-start | bytes 8519680 | tf_op jit(solution)/shard_map/psum | solution.py:113
  105.0 1.1 copy-start
  105.0 1.4 copy-start.1
  105.2 1.5 copy-start.4
  109.4 0.9 copy-start.6
  109.7 7.2 %copy-start.5 = (f32[128]{0:T(128)S(1)}, f32[128]{0:T(128)}, u32[]{:S(2)}) copy-start(f32[128]{0:T(128)} %param.12) | copy-start | bytes 1540
  109.7 7.2 %copy-start.3 = (bf16[128,400]{0,1:T(8,128)(2,1)S(1)}, bf16[128,400]{0,1:T(8,128)(2,1)}, u32[]{:S(2)}) copy-start(bf16[128,400]{0,1:T(8,128)(2,1)} %param.11) | copy-start | bytes 307204
  110.4 7.1 %collective-permute-start = (bf16[128,400]{0,1:T(8,128)(2,1)S(1)}, bf16[128,400]{0,1:T(8,128)(2,1)S(1)}, u32[]{:S(2)}, u32[]{:S(2)}) collective-permute-start(bf16[128,400]{0,1:T(8,128)(2,1)S(1)} %fusion.32), channel_id=1, source_target_pairs={{0,1},{1,2},{2,3},{3,4},{4,5},{5,6},{6,7},{7,8},{8,9},{9,10},{10,1... | collective-permute-start | bytes 307208 | tf_op jit(solution)/shard_map/ppermute | solution.py:13
  113.9 20.7 %collective-permute-start.1 = (f32[128]{0:T(128)S(1)}, f32[128]{0:T(128)S(1)}, u32[]{:S(2)}, u32[]{:S(2)}) collective-permute-start(f32[128]{0:T(128)S(1)} %get-tuple-element.13), channel_id=1, source_target_pairs={{0,1},{1,2},{2,3},{3,4},{4,5},{5,6},{6,7},{7,8},{8,9},{9,10},{10,1... | collective-permute-start | bytes 1544 | tf_op jit(solution)/shard_map/ppermute | solution.py:13
  118.5 1.7 copy-start.8
  132.3 1.2 copy-start.9
  133.9 487.7 %copy-start.7 = (f32[65]{0:T(128)S(1)}, f32[65]{0:T(128)}, u32[]{:S(2)}) copy-start(f32[65]{0:T(128)} %param.16) | copy-start | bytes 784
  133.9 488.2 %copy-start.2 = (f32[65,400]{1,0:T(8,128)S(1)}, f32[65,400]{1,0:T(8,128)}, u32[]{:S(2)}) copy-start(f32[65,400]{1,0:T(8,128)} %param.15) | copy-start | bytes 312004
Sparse Core Ops, SparseCore 0:
  11.7 86.0 all-gather.2
  132.4 488.1 all-reduce.1
where the time goes:
time: 632 us; the launch traced here: 631 us
  waiting for transfers between devices  561 us (89%)
  other arithmetic  21.4 us (3%)
  local copies, waits for them, and re-layouts  15.5 us (2%)
  between operations  14.4 us (2%)
  matrix products  12.1 us (2%)
    psum x1, waiting for transfers between devices, body(): whole = lax.psum(accum, ('grp', 'dev'))  483 us
    all_gather x1, waiting for transfers between devices, body(): lax.all_gather(relations.astype(jnp.bfloat16), 'dev', axis=0, tiled=True)  78.3 us
  transfers between devices with their start and end apart: 4, of which 2 were waited for; matrix products, arithmetic and copies ran while one was open for 5% of the time, Pallas kernels for 0%

commit v1 on v0

v1 whole, which is shorter than its diff:
```python
import functools

import jax
import jax.numpy as jnp
from jax import lax
from jax.experimental import pallas as pl
from jax.experimental.pallas import tpu as pltpu
from jax.sharding import PartitionSpec as P

LEARN = 0.1
EPSILON = 1e-06
MESH = pl.DeviceIdType.MESH
F32, BF16, I32 = jnp.float32, jnp.bfloat16, jnp.int32

D = 400
HALF = 200
WIDE = 512
OWN = 65
ROWS = 80
EP = 128
SLOTS = 512
LANE = 128


def flip(value, k):
    if k == 1:
        return value + 1 - 2 * (value % 2)
    if k == 3:
        return 3 - value
    return (value + 2) % 4


def dot(a, b, ca, cb):
    return lax.dot_general(a, b, (((ca,), (cb,)), ((), ())), preferred_element_type=F32)


def hot(index, first, count):
    rows = lax.broadcasted_iota(I32, (count, index.shape[1]), 0) + first
    return jnp.where(rows == index, 1.0, 0.0).astype(BF16)


def split(value):
    high = value.astype(BF16)
    return high, (value - high.astype(F32)).astype(BF16)


def adagrad(rows, state, grad):
    new_state = state + jnp.sum(grad * grad, axis=0, keepdims=True) / D
    moved = rows.astype(F32) - LEARN * grad / (jnp.sqrt(new_state) + EPSILON)
    return moved.astype(BF16), new_state


def kernel(
    lhs_ref, lst_ref, rhs_ref, rst_ref, rel_ref, relst_ref, src_ref, dst_ref, kind_ref, neg_ref, count_ref,
    lhs_out, lst_out, rhs_out, rst_out, rel_out, relst_out,
    table, hot_all, hot_mine, kinds, a_buf, rr_buf, q_buf, m_hi, m_lo, edges,
    rhs_send, rst_send, rhs_in, rst_in, part, x_in, y_in, x2_in, y2_in, z_out, z_in, low, full, stage2x, stage2y,
    send_sem, recv_sem,
):
    grp, dev = lax.axis_index("grp"), lax.axis_index("dev")
    y, zl = grp // 4, grp % 4
    zh, x, c = dev // 8, (dev // 2) % 4, dev % 2

    def place(x_=None, y_=None, zh_=None, zl_=None, c_=None):
        x_ = x if x_ is None else x_
        y_ = y if y_ is None else y_
        zh_ = zh if zh_ is None else zh_
        zl_ = zl if zl_ is None else zl_
        c_ = c if c_ is None else c_
        return (y_ * 4 + zl_, zh_ * 8 + x_ * 2 + c_)

    sibling = place(c_=1 - c)
    after = (grp, (dev + 1) % 32)
    before = (grp, (dev + 31) % 32)
    ks = (1, 3, 2)
    xs = {k: place(x_=flip(x, k)) for k in ks}
    ys = {k: place(y_=flip(y, k)) for k in ks}
    zhs = {k: place(zh_=flip(zh, k)) for k in ks}
    zls = {k: place(zl_=flip(zl, k)) for k in ks}

    barrier = pltpu.get_barrier_semaphore()
    greet = [sibling, before, *xs.values(), *ys.values(), *zhs.values(), *zls.values()]
    for other in greet:
        pl.semaphore_signal(barrier, inc=1, device_id=other, device_id_type=MESH)

    started = []

    def send(src, dst, target):
        i = len(started)
        copy = pltpu.make_async_remote_copy(
            src_ref=src, dst_ref=dst, send_sem=send_sem.at[i], recv_sem=recv_sem.at[i],
            device_id=target, device_id_type=MESH,
        )
        copy.start()
        started.append(copy)
        return copy

    def arrived(copies):
        for copy in copies:
            copy.wait_recv()

    def lane(value):
        return pl.ds(pl.multiple_of(value * LANE, LANE), LANE)

    table[zh, x, c] = jnp.zeros((ROWS, WIDE), BF16)
    table[zh, x, c, 0:OWN, 0:D] = rel_ref[...].astype(BF16)
    kinds[c] = jnp.concatenate([kind_ref[0], jnp.zeros((6, SLOTS), I32)], axis=0)
    own_slots = pl.ds(pl.multiple_of(c * 2 * SLOTS, 2 * SLOTS), 2 * SLOTS)
    edges[D:WIDE, own_slots] = jnp.zeros((WIDE - D, 2 * SLOTS), BF16)

    pl.semaphore_wait(barrier, len(greet))

    mine = table.at[zh, x, c]
    quarter = table.at[zh, x, c, :, lane(y)]
    to_zh = {k: send(quarter, quarter, zhs[k]) for k in ks}
    own_x = [send(mine, mine, xs[k]) for k in ks]
    kinds_sib = send(kinds.at[c], kinds.at[c], sibling)

    both = jnp.concatenate([kind_ref[0, 0:1, :], kind_ref[0, 1:2, :]], axis=1)
    shard_of = (both * 64528) >> 22
    spot = both + (ROWS - OWN) * shard_of

    def fill(i, _):
        hot_all[i // 8, pl.ds(pl.multiple_of((i % 8) * ROWS, ROWS), ROWS), :] = hot(spot, i * ROWS, ROWS)
        return 0

    lax.fori_loop(0, 32, fill, 0)

    def spread_y_first(k, lo, hi):
        other = flip(zh, k)
        piece = table.at[other, x, c, lo:hi, lane(y)]
        return [send(piece, piece, ys[j]) for j in ks]

    def spread_y_second(k, lo, hi):
        other = flip(zh, k)
        piece = table.at[other, :, c, lo:hi, lane(y)]
        return [send(piece, piece, ys[j]) for j in ks]

    def spread_x_first(k, lo, hi):
        other = flip(zh, k)
        piece = table.at[other, x, c, lo:hi, lane(y)]
        return [send(piece, piece, xs[j]) for j in ks]

    def spread_x_second(k, lo, hi):
        other = flip(zh, k)
        piece = table.at[other, x, c, lo:hi, :]
        return [send(piece, piece, xs[j]) for j in ks]

    def to_sibling(where):
        piece = table.at[where, :, c]
        return send(piece, piece, sibling)

    def look_up(where, first):
        got = dot(table[where].reshape(8 * ROWS, WIDE)[:, 0:D], hot_all[where], 0, 0)
        if first:
            rr_buf[...] = got
        else:
            rr_buf[...] += got

    cut = 48
    arrived([to_zh[1]])
    one_a = spread_y_first(1, 0, ROWS)
    arrived([to_zh[3]])
    three_a = spread_x_first(3, 0, ROWS)
    arrived(own_x)
    sib_own = to_sibling(zh)
    arrived([to_zh[2]])
    two_x = spread_x_first(2, 0, cut)
    two_y = spread_y_first(2, cut, ROWS)
    arrived(one_a)
    one_b = spread_x_second(1, 0, ROWS)
    arrived(three_a)
    three_b = spread_y_second(3, 0, ROWS)
    arrived([sib_own])
    look_up(zh, True)
    arrived(two_x)
    two_xb = spread_y_second(2, 0, cut)
    arrived(two_y)
    two_yb = spread_x_second(2, cut, ROWS)
    arrived(one_b)
    sib_one = to_sibling(flip(zh, 1))
    arrived(three_b)
    sib_three = to_sibling(flip(zh, 3))
    arrived([sib_one])
    look_up(flip(zh, 1), False)
    arrived(two_xb)
    arrived(two_yb)
    sib_two = to_sibling(flip(zh, 2))
    arrived([sib_three])
    look_up(flip(zh, 3), False)
    arrived([sib_two])
    look_up(flip(zh, 2), False)

    def front(turn, lhs):
        src = hot(src_ref[0, turn : turn + 1, :], 0, EP)
        a_buf[...] = dot(lhs, src, 1, 0)
        cols = slice(turn * SLOTS, (turn + 1) * SLOTS)
        a_re, a_im = a_buf[0:HALF, :], a_buf[HALF:D, :]
        r_re, r_im = rr_buf[0:HALF, cols], rr_buf[HALF:D, cols]
        q_buf[...] = jnp.concatenate([a_re * r_re - a_im * r_im, a_re * r_im + a_im * r_re], axis=0).astype(BF16)

    def weights(turn, rhs):
        score = dot(rhs, q_buf[...], 0, 0)
        dst = dst_ref[0, turn : turn + 1, :]
        is_dst = lax.broadcasted_iota(I32, (EP, SLOTS), 0) == dst
        drawn = hot(neg_ref[0, turn : turn + 1, :], 0, EP)
        times = jnp.sum(drawn.astype(F32), axis=1, keepdims=True)
        pos = jnp.sum(jnp.where(is_dst, score, 0.0), axis=0, keepdims=True)
        live = jnp.where(
            lax.broadcasted_iota(I32, (1, SLOTS), 1) < count_ref[0, turn], 1.0, 0.0
        )
        neg_exp = jnp.exp(score)
        pos_exp = jnp.exp(pos)
        total = pos_exp + jnp.sum(jnp.where(times > 0.0, times * neg_exp, 0.0), axis=0, keepdims=True)
        w_pos = live * (pos_exp / total - 1.0)
        w_neg = (live * neg_exp / total).astype(BF16).astype(F32)
        weight = jnp.where(times > 0.0, times * w_neg, 0.0) + jnp.where(is_dst, w_pos, 0.0)
        high, rest = split(weight)
        m_hi[...] = high
        m_lo[...] = rest

    def rhs_grad():
        q = q_buf[...]
        return dot(q, m_hi[...], 1, 1) + dot(q, m_lo[...], 1, 1)

    def back(turn, rhs):
        dq = dot(rhs, m_hi[...], 1, 0) + dot(rhs, m_lo[...], 1, 0)
        cols = slice(turn * SLOTS, (turn + 1) * SLOTS)
        d_re, d_im = dq[0:HALF, :], dq[HALF:D, :]
        a_re, a_im = a_buf[0:HALF, :], a_buf[HALF:D, :]
        r_re, r_im = rr_buf[0:HALF, cols], rr_buf[HALF:D, cols]
        grad_r = jnp.concatenate([d_re * a_re + d_im * a_im, d_im * a_re - d_re * a_im], axis=0)
        a_buf[...] = jnp.concatenate([d_re * r_re + d_im * r_im, d_im * r_re - d_re * r_im], axis=0)
        spot_ = pl.ds(pl.multiple_of((c * 2 + turn) * SLOTS, SLOTS), SLOTS)
        edges[0:D, spot_] = grad_r.astype(BF16)
        return send(edges.at[:, spot_], edges.at[:, spot_], sibling)

    def lhs_grad(turn):
        src = hot(src_ref[0, turn : turn + 1, :], 0, EP)
        high, rest = split(a_buf[...])
        return dot(high, src, 1, 1) + dot(rest, src, 1, 1)

    front(0, lhs_ref[...])
    weights(0, rhs_ref[...])
    new_rhs, new_rst = adagrad(rhs_ref[...], rst_ref[...], rhs_grad())
    rhs_send[...] = new_rhs
    rst_send[...] = jnp.broadcast_to(new_rst, (8, EP))
    passed = [send(rhs_send, rhs_in, after), send(rst_send, rst_in, after)]
    edges_sib = [back(0, rhs_ref[...])]
    new_lhs, new_lst = adagrad(lhs_ref[...], lst_ref[...], lhs_grad(0))
    lhs_out[...] = new_lhs
    lst_out[...] = new_lst

    front(1, lhs_out[...])

    arrived([kinds_sib])
    for core in range(2):
        for turn in range(2):
            kind = kinds[core, turn : turn + 1, :]
            shard = (kind * 64528) >> 22
            half = shard >> 1
            local = jnp.where(shard - 2 * half == c, kind - OWN * shard + ROWS * half, -1)
            at = (core * 2 + turn) * SLOTS

            def fill_mine(i, _, local=local, at=at):
                hot_mine[i // 4, pl.ds(pl.multiple_of((i % 4) * ROWS, ROWS), ROWS), at : at + SLOTS] = hot(
                    local, i * ROWS, ROWS
                )
                return 0

            lax.fori_loop(0, 16, fill_mine, 0)

    arrived(passed)
    weights(1, rhs_in[...])
    edges_sib.append(back(1, rhs_in[...]))
    arrived(edges_sib)

    def chunk(i):
        got = dot(hot_mine[i], edges[...], 1, 1)
        part[i] = got.astype(BF16).reshape(4, ROWS, WIDE)

    chunk(0)
    chunk(1)
    xa = {k: send(part.at[0:2, flip(x, k)], x_in.at[k - 1], xs[k]) for k in ks}
    chunk(2)
    chunk(3)
    ya = {k: send(part.at[2:4, :, :, lane(flip(y, k))], y_in.at[k - 1], ys[k]) for k in ks}

    new_rhs, new_rst = adagrad(rhs_in[...], rst_in[0:1, :], rhs_grad())
    rhs_out[...] = new_rhs
    rst_out[...] = new_rst
    new_lhs, new_lst = adagrad(lhs_out[...], lst_out[...], lhs_grad(1))
    lhs_out[...] = new_lhs
    lst_out[...] = new_lst

    arrived(xa.values())
    sum_x = part[0:2, x].astype(F32)
    for k in ks:
        sum_x += x_in[k - 1].astype(F32)
    stage2y[...] = sum_x.astype(BF16)
    yb = {k: send(stage2y.at[:, :, lane(flip(y, k))], y2_in.at[k - 1], ys[k]) for k in ks}

    arrived(ya.values())
    sum_y = part[2:4, :, :, lane(y)].astype(F32)
    for k in ks:
        sum_y += y_in[k - 1].astype(F32)
    stage2x[...] = sum_y.astype(BF16)
    xb = {k: send(stage2x.at[:, flip(x, k)], x2_in.at[k - 1], xs[k]) for k in ks}

    arrived(yb.values())
    low_sum = stage2y[:, :, lane(y)].astype(F32)
    for k in ks:
        low_sum += y2_in[k - 1].astype(F32)
    z_out[0:2] = low_sum.astype(BF16)
    arrived(xb.values())
    high_sum = stage2x[:, x].astype(F32)
    for k in ks:
        high_sum += x2_in[k - 1].astype(F32)
    z_out[2:4] = high_sum.astype(BF16)

    za = {k: send(z_out.at[flip(zh, k)], z_in.at[k - 1], zhs[k]) for k in ks}
    arrived(za.values())
    over_zh = z_out[zh].astype(F32)
    for k in ks:
        over_zh += z_in[k - 1].astype(F32)
    low[zl] = over_zh.astype(BF16)
    zb = [send(low.at[zl], low.at[zl], zls[k]) for k in ks]
    arrived(zb)
    both_z = (low[0].astype(F32) + low[1].astype(F32)) + (low[2].astype(F32) + low[3].astype(F32))
    full[:, lane(y)] = both_z
    last = [send(full.at[:, lane(y)], full.at[:, lane(y)], ys[k]) for k in ks]
    arrived(last)

    total = full[0:OWN, 0:D]
    eye = lax.broadcasted_iota(I32, (OWN, OWN), 0) == lax.broadcasted_iota(I32, (OWN, OWN), 1)
    old = jnp.sum(jnp.where(eye, relst_ref[...], 0.0), axis=1, keepdims=True)
    new = old + jnp.sum(total * total, axis=1, keepdims=True) / D
    rel_out[...] = rel_ref[...] - LEARN * total / (jnp.sqrt(new) + EPSILON)
    relst_out[...] = jnp.sum(jnp.where(eye, new, 0.0), axis=0, keepdims=True)

    for copy in started:
        copy.wait_send()


N_COPIES = 80


def body(
    lhs_table, lhs_state, rhs_table, rhs_state, relations, rel_state,
    src_index, dst_index, rel_index, neg_index, edge_count,
):
    vmem = pl.BlockSpec(memory_space=pltpu.VMEM)
    smem = pl.BlockSpec(memory_space=pltpu.SMEM)
    shape = jax.ShapeDtypeStruct
    outs = pl.pallas_call(
        kernel,
        out_shape=(
            shape((D, EP), BF16), shape((1, EP), F32), shape((D, EP), BF16), shape((1, EP), F32),
            shape((OWN, D), F32), shape((1, OWN), F32),
        ),
        in_specs=[vmem] * 10 + [smem],
        out_specs=(vmem,) * 6,
        scratch_shapes=[
            pltpu.VMEM((4, 4, 2, ROWS, WIDE), BF16),
            pltpu.VMEM((4, 8 * ROWS, 2 * SLOTS), BF16),
            pltpu.VMEM((4, 4 * ROWS, 4 * SLOTS), BF16),
            pltpu.VMEM((2, 8, SLOTS), I32),
            pltpu.VMEM((D, SLOTS), F32),
            pltpu.VMEM((D, 2 * SLOTS), F32),
            pltpu.VMEM((D, SLOTS), BF16),
            pltpu.VMEM((EP, SLOTS), BF16),
            pltpu.VMEM((EP, SLOTS), BF16),
            pltpu.VMEM((WIDE, 4 * SLOTS), BF16),
            pltpu.VMEM((D, EP), BF16),
            pltpu.VMEM((8, EP), F32),
            pltpu.VMEM((D, EP), BF16),
            pltpu.VMEM((8, EP), F32),
            pltpu.VMEM((4, 4, ROWS, WIDE), BF16),
            pltpu.VMEM((3, 2, ROWS, WIDE), BF16),
            pltpu.VMEM((3, 2, 4, ROWS, LANE), BF16),
            pltpu.VMEM((3, 2, ROWS, LANE), BF16),
            pltpu.VMEM((3, 2, ROWS, LANE), BF16),
            pltpu.VMEM((4, ROWS, LANE), BF16),
            pltpu.VMEM((3, ROWS, LANE), BF16),
            pltpu.VMEM((4, ROWS, LANE), BF16),
            pltpu.VMEM((ROWS, WIDE), F32),
            pltpu.VMEM((2, 4, ROWS, LANE), BF16),
            pltpu.VMEM((2, ROWS, WIDE), BF16),
            pltpu.SemaphoreType.DMA((N_COPIES,)),
            pltpu.SemaphoreType.DMA((N_COPIES,)),
        ],
        compiler_params=pltpu.CompilerParams(
            collective_id=0, has_side_effects=True, vmem_limit_bytes=48 * 2**20
        ),
        name="train",
    )(
        lhs_table.T, lhs_state[None, :], rhs_table.T, rhs_state[None, :], relations, rel_state[None, :],
        src_index, dst_index, rel_index, neg_index, edge_count,
    )
    lhs, lhs_st, rhs, rhs_st, rel, rel_st = outs
    return (lhs.T, lhs_st[0], rhs.T, rhs_st[0], rel, rel_st[0])


def solution(mesh):
    return jax.shard_map(
        body,
        mesh=mesh,
        in_specs=(
            P(("grp", "dev"), None),
            P(("grp", "dev")),
            P(("grp", "dev"), None),
            P(("grp", "dev")),
            P("dev", None),
            P("dev"),
            P(("grp", "dev"), None, None),
            P(("grp", "dev"), None, None),
            P(("grp", "dev"), None, None),
            P(("grp", "dev"), None, None),
            P(("grp", "dev"), None),
        ),
        out_specs=(
            P(("grp", "dev"), None),
            P(("grp", "dev")),
            P(("grp", "dev"), None),
            P(("grp", "dev")),
            P("dev", None),
            P("dev"),
        ),
        check_vma=False,
    )
```

time: 632 us -> 90.1 us (0.14)
  waiting for transfers between devices: 561 us -> 0 us
  Pallas kernels: 0 us -> 79.6 us
  other arithmetic: 21.4 us -> 0 us
  between operations: 14.4 us -> 0.69 us
  matrix products: 12.1 us -> 0 us
    psum x1 -> x0, waiting for transfers between devices: 483 us -> none  [body(): whole = lax.psum(accum, ('grp', 'dev'))]
    pallas_call x0 -> x1, Pallas kernels: none -> 79.6 us  [body(): pl.pallas_call(kernel, out_shape=(shape((D, EP), BF16), shape((1, EP), F3...]
    all_gather x1 -> x0, waiting for transfers between devices: 78.3 us -> none  [body(): lax.all_gather(relations.astype(jnp.bfloat16), 'dev', axis=0, tiled=True)]
    add x10 -> x0, other arithmetic: 12.9 us -> none  [the longest x1 9.44 us: body(): accum = accum + grads]
    dot_general x18 -> x0, matrix products: 12.1 us -> none  [the longest x6 3.72 us: spread_rows(): lax.dot_general(hot.astype(jnp.float32), grad, (((0,), (0,)), ((), ())),...]
  transfers between devices with their start and end apart: 4 -> 0, of which waited for: 2 -> 0; matrix products, arithmetic and copies ran while one was open for 5% -> 0% of each run, Pallas kernels for 0% -> 0%
where the time goes in v1:
time: 90.1 us; the launch traced here: 89.8 us
  Pallas kernels  79.6 us (88%)
  local copies, waits for them, and re-layouts  9.54 us (11%)
    pallas_call x1, Pallas kernels, body(): pl.pallas_call(kernel, out_shape=(shape((D, EP), BF16), shape((1, EP), F3...  79.6 us
    unnamed x28, local copies, waits for them, and re-layouts  9.54 us

profile of v1, /device:TPU:1, one launch (start us, length us, event | category | flops | bytes accessed | tf_op | source)
XLA Modules:
  0.0 89.8 jit_solution(17306083180661833315)
XLA Ops:
  0.6 0.0 copy-start.4
  0.6 0.0 copy-start.3
  0.7 0.0 copy-start.7
  0.7 0.0 copy-start.8
  0.7 0.6 copy-done.4
  1.3 0.0 copy-done.3
  1.3 0.0 copy-done.7
  1.3 0.0 copy-done.8
  1.3 0.0 copy-start
  1.3 0.9 %copy-done = f32[65,400]{1,0:T(8,128)S(1)} copy-done((f32[65,400]{1,0:T(8,128)S(1)}, f32[65,400]{1,0:T(8,128)}, u32[]{:S(2)}) %copy-start) | copy-done | bytes 104024
  2.3 0.0 copy-start.1
  2.3 0.9 copy-done.1
  3.2 0.0 copy-start.2
  3.2 0.9 copy-done.2
  4.0 0.0 copy-start.5
  4.0 0.7 copy-done.5
  4.7 0.0 copy-start.6
  4.7 0.7 copy-done.6
  5.4 0.0 copy-start.9
  5.4 0.7 copy-done.9
  6.1 0.0 copy-start.10
  6.1 0.7 copy-done.10
  6.7 79.6 %train.1 = (bf16[400,128]{1,0:T(8,128)(2,1)S(1)}, f32[1,128]{1,0:T(1,128)S(1)}, bf16[400,128]{1,0:T(8,128)(2,1)S(1)}, f32[1,128]{1,0:T(1,128)S(1)}, f32[65,400]{1,0:T(8,128)S(1)}, /*index=5*/f32[1,65]{1,0:T(1,128)S(1)}) custom-call(bf16[400,128]{1,0:T(8,128)(2,1)S(1)} %bitcast.10, f32[1,128]{1,0:T(1,128)S(1)} %bitcast.14, bf16[400,128]{1,0:T(8,128)(2,1)S(1)} %bitcast.11, ...), custom_call_target="tpu_custom_call" | custom-call | tf_op jit(solution)/shard_map/train/pallas_call | solution.py:355
  86.3 0.6 copy.23
  86.9 0.5 copy.24
  87.5 0.6 copy.25
  88.1 0.5 copy.26
  88.6 0.7 copy.27
  89.3 0.5 copy.28
Async XLA Ops:
  0.6 0.7 copy-start.4
  0.6 0.7 copy-start.3
  0.7 0.7 copy-start.7
  0.7 0.7 copy-start.8
  1.3 0.9 %copy-start = (f32[65,400]{1,0:T(8,128)S(1)}, f32[65,400]{1,0:T(8,128)}, u32[]{:S(2)}) copy-start(f32[65,400]{1,0:T(8,128)} %rel_ref.1) | copy-start | bytes 312004
  2.3 0.9 copy-start.1
  3.2 0.9 copy-start.2
  4.0 0.7 copy-start.5
  4.7 0.7 copy-start.6
  5.4 0.7 copy-start.9
  6.1 0.7 copy-start.10

commit v2 on v1

--- a/solution.py
+++ b/solution.py
@@ -51,11 +51,13 @@
 
 
 def kernel(
-    lhs_ref, lst_ref, rhs_ref, rst_ref, rel_ref, relst_ref, src_ref, dst_ref, kind_ref, neg_ref, count_ref,
+    lhs_hbm, lst_hbm, rhs_hbm, rst_hbm, rel_hbm, relst_hbm, src_hbm, dst_hbm, kind_hbm, neg_hbm, count_ref,
+    lhs_res, lst_res, rhs_res, rst_res, rel_res, relst_res,
+    lhs_ref, lst_ref, rhs_ref, rst_ref, rel_ref, relst_ref, src_ref, dst_ref, kind_ref, neg_ref,
     lhs_out, lst_out, rhs_out, rst_out, rel_out, relst_out,
     table, hot_all, hot_mine, kinds, a_buf, rr_buf, q_buf, m_hi, m_lo, edges,
     rhs_send, rst_send, rhs_in, rst_in, part, x_in, y_in, x2_in, y2_in, z_out, z_in, low, full, stage2x, stage2y,
-    send_sem, recv_sem,
+    send_sem, recv_sem, in_sem, out_sem,
 ):
     grp, dev = lax.axis_index("grp"), lax.axis_index("dev")
     y, zl = grp // 4, grp % 4
@@ -83,7 +85,23 @@
     for other in greet:
         pl.semaphore_signal(barrier, inc=1, device_id=other, device_id_type=MESH)
 
-    started = []
+    loads = [
+        pltpu.make_async_copy(src, dst, in_sem.at[i])
+        for i, (src, dst) in enumerate(
+            (
+                (rel_hbm, rel_ref), (kind_hbm, kind_ref), (lhs_hbm, lhs_ref), (src_hbm, src_ref), (rhs_hbm, rhs_ref),
+                (dst_hbm, dst_ref), (neg_hbm, neg_ref), (lst_hbm, lst_ref), (rst_hbm, rst_ref), (relst_hbm, relst_ref),
+            )
+        )
+    ]
+    for copy in loads:
+        copy.start()
+    started, stores = [], []
+
+    def give(src, dst):
+        copy = pltpu.make_async_copy(src, dst, out_sem.at[len(stores)])
+        copy.start()
+        stores.append(copy)
 
     def send(src, dst, target):
         i = len(started)
@@ -102,11 +120,13 @@
     def lane(value):
         return pl.ds(pl.multiple_of(value * LANE, LANE), LANE)
 
+    own_slots = pl.ds(pl.multiple_of(c * 2 * SLOTS, 2 * SLOTS), 2 * SLOTS)
+    edges[D:WIDE, own_slots] = jnp.zeros((WIDE - D, 2 * SLOTS), BF16)
     table[zh, x, c] = jnp.zeros((ROWS, WIDE), BF16)
+    for copy in loads[:2]:
+        copy.wait()
     table[zh, x, c, 0:OWN, 0:D] = rel_ref[...].astype(BF16)
     kinds[c] = jnp.concatenate([kind_ref[0], jnp.zeros((6, SLOTS), I32)], axis=0)
-    own_slots = pl.ds(pl.multiple_of(c * 2 * SLOTS, 2 * SLOTS), 2 * SLOTS)
-    edges[D:WIDE, own_slots] = jnp.zeros((WIDE - D, 2 * SLOTS), BF16)
 
     pl.semaphore_wait(barrier, len(greet))
 
@@ -125,6 +145,8 @@
         return 0
 
     lax.fori_loop(0, 32, fill, 0)
+    for copy in loads[2:]:
+        copy.wait()
 
     def spread_y_first(k, lo, hi):
         other = flip(zh, k)
@@ -279,12 +301,15 @@
         got = dot(hot_mine[i], edges[...], 1, 1)
         part[i] = got.astype(BF16).reshape(4, ROWS, WIDE)
 
-    chunk(0)
-    chunk(1)
-    xa = {k: send(part.at[0:2, flip(x, k)], x_in.at[k - 1], xs[k]) for k in ks}
-    chunk(2)
-    chunk(3)
-    ya = {k: send(part.at[2:4, :, :, lane(flip(y, k))], y_in.at[k - 1], ys[k]) for k in ks}
+    def x_first(i):
+        chunk(i)
+        return {k: send(part.at[i, flip(x, k)], x_in.at[i, k - 1], xs[k]) for k in ks}
+
+    def y_first(i):
+        chunk(i)
+        return {k: send(part.at[i, :, :, lane(flip(y, k))], y_in.at[i - 2, k - 1], ys[k]) for k in ks}
+
+    first = {0: x_first(0), 2: y_first(2), 1: x_first(1), 3: y_first(3)}
 
     new_rhs, new_rst = adagrad(rhs_in[...], rst_in[0:1, :], rhs_grad())
     rhs_out[...] = new_rhs
@@ -292,31 +317,33 @@
     new_lhs, new_lst = adagrad(lhs_out[...], lst_out[...], lhs_grad(1))
     lhs_out[...] = new_lhs
     lst_out[...] = new_lst
-
-    arrived(xa.values())
-    sum_x = part[0:2, x].astype(F32)
-    for k in ks:
-        sum_x += x_in[k - 1].astype(F32)
-    stage2y[...] = sum_x.astype(BF16)
-    yb = {k: send(stage2y.at[:, :, lane(flip(y, k))], y2_in.at[k - 1], ys[k]) for k in ks}
-
-    arrived(ya.values())
-    sum_y = part[2:4, :, :, lane(y)].astype(F32)
-    for k in ks:
-        sum_y += y_in[k - 1].astype(F32)
-    stage2x[...] = sum_y.astype(BF16)
-    xb = {k: send(stage2x.at[:, flip(x, k)], x2_in.at[k - 1], xs[k]) for k in ks}
-
-    arrived(yb.values())
-    low_sum = stage2y[:, :, lane(y)].astype(F32)
-    for k in ks:
-        low_sum += y2_in[k - 1].astype(F32)
-    z_out[0:2] = low_sum.astype(BF16)
-    arrived(xb.values())
-    high_sum = stage2x[:, x].astype(F32)
-    for k in ks:
-        high_sum += x2_in[k - 1].astype(F32)
-    z_out[2:4] = high_sum.astype(BF16)
+    for src, dst in ((lhs_out, lhs_res), (lst_out, lst_res), (rhs_out, rhs_res), (rst_out, rst_res)):
+        give(src, dst)
+
+    def x_then_y(i):
+        arrived(first[i].values())
+        total = part[i, x].astype(F32)
+        for k in ks:
+            total += x_in[i, k - 1].astype(F32)
+        stage2y[i] = total.astype(BF16)
+        return {k: send(stage2y.at[i, :, lane(flip(y, k))], y2_in.at[i, k - 1], ys[k]) for k in ks}
+
+    def y_then_x(i):
+        arrived(first[i].values())
+        total = part[i, :, :, lane(y)].astype(F32)
+        for k in ks:
+            total += y_in[i - 2, k - 1].astype(F32)
+        stage2x[i - 2] = total.astype(BF16)
+        return {k: send(stage2x.at[i - 2, flip(x, k)], x2_in.at[i - 2, k - 1], xs[k]) for k in ks}
+
+    second = {0: x_then_y(0), 2: y_then_x(2), 1: x_then_y(1), 3: y_then_x(3)}
+
+    for i in (0, 2, 1, 3):
+        arrived(second[i].values())
+        total = (stage2y[i, :, lane(y)] if i < 2 else stage2x[i - 2, x]).astype(F32)
+        for k in ks:
+            total += (y2_in[i, k - 1] if i < 2 else x2_in[i - 2, k - 1]).astype(F32)
+        z_out[i] = total.astype(BF16)
 
     za = {k: send(z_out.at[flip(zh, k)], z_in.at[k - 1], zhs[k]) for k in ks}
     arrived(za.values())
@@ -338,29 +365,51 @@
     rel_out[...] = rel_ref[...] - LEARN * total / (jnp.sqrt(new) + EPSILON)
     relst_out[...] = jnp.sum(jnp.where(eye, new, 0.0), axis=0, keepdims=True)
 
+    give(rel_out, rel_res)
+    give(relst_out, relst_res)
     for copy in started:
         copy.wait_send()
-
-
-N_COPIES = 80
+    for copy in stores:
+        copy.wait()
+
+
+def hand_on(*refs):
+    held, sem = refs[12:18], refs[18]
+    loads = [pltpu.make_async_copy(refs[i], held[i], sem.at[i]) for i in range(6)]
+    stores = [pltpu.make_async_copy(held[i], refs[6 + i], sem.at[6 + i]) for i in range(6)]
+    for copy in loads:
+        copy.start()
+    for load, store in zip(loads, stores):
+        load.wait()
+        store.start()
+    for copy in stores:
+        copy.wait()
+
+
+N_COPIES = 96
 
 
 def body(
     lhs_table, lhs_state, rhs_table, rhs_state, relations, rel_state,
     src_index, dst_index, rel_index, neg_index, edge_count,
 ):
-    vmem = pl.BlockSpec(memory_space=pltpu.VMEM)
+    hbm = pl.BlockSpec(memory_space=pltpu.HBM)
     smem = pl.BlockSpec(memory_space=pltpu.SMEM)
     shape = jax.ShapeDtypeStruct
+    out_shape = (
+        shape((D, EP), BF16), shape((1, EP), F32), shape((D, EP), BF16), shape((1, EP), F32),
+        shape((OWN, D), F32), shape((1, OWN), F32),
+    )
     outs = pl.pallas_call(
         kernel,
-        out_shape=(
-            shape((D, EP), BF16), shape((1, EP), F32), shape((D, EP), BF16), shape((1, EP), F32),
-            shape((OWN, D), F32), shape((1, OWN), F32),
-        ),
-        in_specs=[vmem] * 10 + [smem],
-        out_specs=(vmem,) * 6,
+        out_shape=out_shape,
+        in_specs=[hbm] * 10 + [smem],
+        out_specs=(hbm,) * 6,
         scratch_shapes=[
+            pltpu.VMEM((D, EP), BF16), pltpu.VMEM((1, EP), F32), pltpu.VMEM((D, EP), BF16), pltpu.VMEM((1, EP), F32),
+            pltpu.VMEM((OWN, D), F32), pltpu.VMEM((1, OWN), F32),
+            *[pltpu.VMEM((1, 2, SLOTS), I32) for _ in range(4)],
+            *[pltpu.VMEM(out.shape, out.dtype) for out in out_shape],
             pltpu.VMEM((4, 4, 2, ROWS, WIDE), BF16),
             pltpu.VMEM((4, 8 * ROWS, 2 * SLOTS), BF16),
             pltpu.VMEM((4, 4 * ROWS, 4 * SLOTS), BF16),
@@ -376,10 +425,10 @@
             pltpu.VMEM((D, EP), BF16),
             pltpu.VMEM((8, EP), F32),
             pltpu.VMEM((4, 4, ROWS, WIDE), BF16),
-            pltpu.VMEM((3, 2, ROWS, WIDE), BF16),
-            pltpu.VMEM((3, 2, 4, ROWS, LANE), BF16),
-            pltpu.VMEM((3, 2, ROWS, LANE), BF16),
-            pltpu.VMEM((3, 2, ROWS, LANE), BF16),
+            pltpu.VMEM((2, 3, ROWS, WIDE), BF16),
+            pltpu.VMEM((2, 3, 4, ROWS, LANE), BF16),
+            pltpu.VMEM((2, 3, ROWS, LANE), BF16),
+            pltpu.VMEM((2, 3, ROWS, LANE), BF16),
             pltpu.VMEM((4, ROWS, LANE), BF16),
             pltpu.VMEM((3, ROWS, LANE), BF16),
             pltpu.VMEM((4, ROWS, LANE), BF16),
@@ -388,16 +437,26 @@
             pltpu.VMEM((2, ROWS, WIDE), BF16),
             pltpu.SemaphoreType.DMA((N_COPIES,)),
             pltpu.SemaphoreType.DMA((N_COPIES,)),
+            pltpu.SemaphoreType.DMA((10,)),
+            pltpu.SemaphoreType.DMA((6,)),
         ],
         compiler_params=pltpu.CompilerParams(
-            collective_id=0, has_side_effects=True, vmem_limit_bytes=48 * 2**20
+            collective_id=0, has_side_effects=True, vmem_limit_bytes=60 * 2**20
         ),
         name="train",
     )(
         lhs_table.T, lhs_state[None, :], rhs_table.T, rhs_state[None, :], relations, rel_state[None, :],
         src_index, dst_index, rel_index, neg_index, edge_count,
     )
-    lhs, lhs_st, rhs, rhs_st, rel, rel_st = outs
+    lhs, lhs_st, rhs, rhs_st, rel, rel_st = pl.pallas_call(
+        hand_on,
+        out_shape=out_shape,
+        in_specs=[hbm] * 6,
+        out_specs=(hbm,) * 6,
+        scratch_shapes=[*[pltpu.VMEM(out.shape, out.dtype) for out in out_shape], pltpu.SemaphoreType.DMA((12,))],
+        compiler_params=pltpu.CompilerParams(vmem_limit_bytes=60 * 2**20),
+        name="hand_on",
+    )(*outs)
     return (lhs.T, lhs_st[0], rhs.T, rhs_st[0], rel, rel_st[0])
 
 

time: 90.1 us -> 82.2 us (0.912)
  local copies, waits for them, and re-layouts: 9.54 us -> 0 us
  Pallas kernels: 79.6 us -> 80.9 us
    unnamed x28 -> x0, local copies, waits for them, and re-layouts: 9.54 us -> none
    pallas_call x1 -> x2, Pallas kernels: 79.6 us -> 80.9 us  [the longest x1 79.1 us: body(): pl.pallas_call(kernel, out_shape=out_shape, in_specs=[hbm] * 10 + [smem],...]
where the time goes in v2:
time: 82.2 us; the launch traced here: 81.5 us
  Pallas kernels  80.9 us (98%)
    pallas_call x1, Pallas kernels, body(): pl.pallas_call(kernel, out_shape=out_shape, in_specs=[hbm] * 10 + [smem],...  79.1 us
    pallas_call x1, Pallas kernels, body(): pl.pallas_call(hand_on, out_shape=out_shape, in_specs=[hbm] * 6, out_spec...  1.79 us

profile of v2, /device:TPU:1, one launch (start us, length us, event | category | flops | bytes accessed | tf_op | source)
XLA Modules:
  0.0 81.5 jit_solution(9979315618222416242)
XLA Ops:
  0.6 79.1 %train.1 = (bf16[400,128]{1,0:T(8,128)(2,1)}, f32[1,128]{1,0:T(1,128)}, bf16[400,128]{1,0:T(8,128)(2,1)}, f32[1,128]{1,0:T(1,128)}, f32[65,400]{1,0:T(8,128)}, /*index=5*/f32[1,65]{1,0:T(1,128)}) custom-call(bf16[400,128]{1,0:T(8,128)(2,1)} %bitcast.10, f32[1,128]{1,0:T(1,128)} %bitcast.12, bf16[400,128]{1,0:T(8,128)(2,1)} %bitcast.11, f32[1,128]{1,0:T(1,128)} %bitcast.13, ...), custom_call_target="tpu_custom_call" | custom-call | tf_op jit(solution)/shard_map/train/pallas_call | solution.py:403
  79.8 1.8 %hand_on.1 = (bf16[400,128]{1,0:T(8,128)(2,1)}, f32[1,128]{1,0:T(1,128)}, bf16[400,128]{1,0:T(8,128)(2,1)}, f32[1,128]{1,0:T(1,128)}, f32[65,400]{1,0:T(8,128)}, /*index=5*/f32[1,65]{1,0:T(1,128)}) custom-call(bf16[400,128]{1,0:T(8,128)(2,1)} %get-tuple-element.18.refs_0_, f32[1,128]{1,0:T(1,128)} %get-tuple-element.19.refs_1_, ...), custom_call_target="tpu_custom_call" | custom-call | tf_op jit(solution)/shard_map/hand_on/pallas_call | solution.py:451

commit v3 on v2

--- a/solution.py
+++ b/solution.py
@@ -73,7 +73,6 @@
 
     sibling = place(c_=1 - c)
     after = (grp, (dev + 1) % 32)
-    before = (grp, (dev + 31) % 32)
     ks = (1, 3, 2)
     xs = {k: place(x_=flip(x, k)) for k in ks}
     ys = {k: place(y_=flip(y, k)) for k in ks}
@@ -81,7 +80,7 @@
     zls = {k: place(zl_=flip(zl, k)) for k in ks}
 
     barrier = pltpu.get_barrier_semaphore()
-    greet = [sibling, before, *xs.values(), *ys.values(), *zhs.values(), *zls.values()]
+    greet = [sibling, *xs.values(), *ys.values(), zhs[1], zhs[3], *zls.values()]
     for other in greet:
         pl.semaphore_signal(barrier, inc=1, device_id=other, device_id_type=MESH)
 
@@ -132,7 +131,7 @@
 
     mine = table.at[zh, x, c]
     quarter = table.at[zh, x, c, :, lane(y)]
-    to_zh = {k: send(quarter, quarter, zhs[k]) for k in ks}
+    to_zh = {k: send(quarter, quarter, zhs[k]) for k in (1, 3)}
     own_x = [send(mine, mine, xs[k]) for k in ks]
     kinds_sib = send(kinds.at[c], kinds.at[c], sibling)
 
@@ -167,6 +166,10 @@
         other = flip(zh, k)
         piece = table.at[other, x, c, lo:hi, :]
         return [send(piece, piece, xs[j]) for j in ks]
+
+    def relay(source, target, lo, hi):
+        piece = table.at[flip(zh, source), x, c, lo:hi, lane(y)]
+        return send(piece, piece, zhs[target])
 
     def to_sibling(where):
         piece = table.at[where, :, c]
@@ -181,13 +184,16 @@
 
     cut = 48
     arrived([to_zh[1]])
+    relay_x = relay(1, 3, 0, cut)
     one_a = spread_y_first(1, 0, ROWS)
     arrived([to_zh[3]])
+    relay_y = relay(3, 1, cut, ROWS)
     three_a = spread_x_first(3, 0, ROWS)
     arrived(own_x)
     sib_own = to_sibling(zh)
-    arrived([to_zh[2]])
+    arrived([relay_x])
     two_x = spread_x_first(2, 0, cut)
+    arrived([relay_y])
     two_y = spread_y_first(2, cut, ROWS)
     arrived(one_a)
     one_b = spread_x_second(1, 0, ROWS)

time: 82.2 us -> 81.9 us (level)
  no operation moved by 1% of the time
where the time goes in v3:
time: 81.9 us; the launch traced here: 81.8 us
  Pallas kernels  81.1 us (99%)
    pallas_call x1, Pallas kernels, body(): pl.pallas_call(kernel, out_shape=out_shape, in_specs=[hbm] * 10 + [smem],...  79.3 us
    pallas_call x1, Pallas kernels, body(): pl.pallas_call(hand_on, out_shape=out_shape, in_specs=[hbm] * 6, out_spec...  1.79 us

profile of v3, /device:TPU:1, one launch (start us, length us, event | category | flops | bytes accessed | tf_op | source)
XLA Modules:
  0.0 81.8 jit_solution(3213956751654861950)
XLA Ops:
  0.6 79.3 %train.1 = (bf16[400,128]{1,0:T(8,128)(2,1)}, f32[1,128]{1,0:T(1,128)}, bf16[400,128]{1,0:T(8,128)(2,1)}, f32[1,128]{1,0:T(1,128)}, f32[65,400]{1,0:T(8,128)}, /*index=5*/f32[1,65]{1,0:T(1,128)}) custom-call(bf16[400,128]{1,0:T(8,128)(2,1)} %bitcast.10, f32[1,128]{1,0:T(1,128)} %bitcast.12, bf16[400,128]{1,0:T(8,128)(2,1)} %bitcast.11, f32[1,128]{1,0:T(1,128)} %bitcast.13, ...), custom_call_target="tpu_custom_call" | custom-call | tf_op jit(solution)/shard_map/train/pallas_call | solution.py:409
  80.0 1.8 %hand_on.1 = (bf16[400,128]{1,0:T(8,128)(2,1)}, f32[1,128]{1,0:T(1,128)}, bf16[400,128]{1,0:T(8,128)(2,1)}, f32[1,128]{1,0:T(1,128)}, f32[65,400]{1,0:T(8,128)}, /*index=5*/f32[1,65]{1,0:T(1,128)}) custom-call(bf16[400,128]{1,0:T(8,128)(2,1)} %get-tuple-element.18.refs_0_, f32[1,128]{1,0:T(1,128)} %get-tuple-element.19.refs_1_, ...), custom_call_target="tpu_custom_call" | custom-call | tf_op jit(solution)/shard_map/hand_on/pallas_call | solution.py:457

commit v4 on v2

--- a/solution.py
+++ b/solution.py
@@ -16,7 +16,8 @@
 HALF = 200
 WIDE = 512
 OWN = 65
-ROWS = 80
+ROWS = 64
+MAIN = 384
 EP = 128
 SLOTS = 512
 LANE = 128
@@ -44,6 +45,24 @@
     return high, (value - high.astype(F32)).astype(BF16)
 
 
+def fold(tail):
+    total = tail[0:8]
+    for i in range(1, 8):
+        total += pltpu.roll(tail[8 * i : 8 * i + 8], 16 * i, 1)
+    return total
+
+
+def unfold(folded, shards):
+    flat = folded.reshape(shards * 8, LANE)
+    groups = [flat if i == 0 else pltpu.roll(flat, LANE - 16 * i, 1) for i in range(8)]
+    return jnp.stack([group.reshape(shards, 8, LANE) for group in groups], axis=1).reshape(shards, ROWS, LANE)
+
+
+def place_of(kind):
+    shard = (kind * 64528) >> 22
+    return shard, kind - OWN * shard
+
+
 def adagrad(rows, state, grad):
     new_state = state + jnp.sum(grad * grad, axis=0, keepdims=True) / D
     moved = rows.astype(F32) - LEARN * grad / (jnp.sqrt(new_state) + EPSILON)
@@ -55,8 +74,8 @@
     lhs_res, lst_res, rhs_res, rst_res, rel_res, relst_res,
     lhs_ref, lst_ref, rhs_ref, rst_ref, rel_ref, relst_ref, src_ref, dst_ref, kind_ref, neg_ref,
     lhs_out, lst_out, rhs_out, rst_out, rel_out, relst_out,
-    table, hot_all, hot_mine, kinds, a_buf, rr_buf, q_buf, m_hi, m_lo, edges,
-    rhs_send, rst_send, rhs_in, rst_in, part, x_in, y_in, x2_in, y2_in, z_out, z_in, low, full, stage2x, stage2y,
+    table, left, spare, hot_all, hot_spare, hot_mine, hot_mine_spare, kinds, wide, a_buf, rr_buf, q_buf, m_hi, m_lo, edges,
+    rhs_send, rst_send, rhs_in, rst_in, part, part_left, l_in, l_y, x_in, y_in, x2_in, y2_in, z_out, z_in, low, full, stage2x, stage2y,
     send_sem, recv_sem, in_sem, out_sem,
 ):
     grp, dev = lax.axis_index("grp"), lax.axis_index("dev")
@@ -73,7 +92,6 @@
 
     sibling = place(c_=1 - c)
     after = (grp, (dev + 1) % 32)
-    before = (grp, (dev + 31) % 32)
     ks = (1, 3, 2)
     xs = {k: place(x_=flip(x, k)) for k in ks}
     ys = {k: place(y_=flip(y, k)) for k in ks}
@@ -81,7 +99,7 @@
     zls = {k: place(zl_=flip(zl, k)) for k in ks}
 
     barrier = pltpu.get_barrier_semaphore()
-    greet = [sibling, before, *xs.values(), *ys.values(), *zhs.values(), *zls.values()]
+    greet = [sibling, *xs.values(), *ys.values(), zhs[1], zhs[3], *zls.values()]
     for other in greet:
         pl.semaphore_signal(barrier, inc=1, device_id=other, device_id_type=MESH)
 
@@ -117,28 +135,34 @@
         for copy in copies:
             copy.wait_recv()
 
-    def lane(value):
-        return pl.ds(pl.multiple_of(value * LANE, LANE), LANE)
+    def rows(value):
+        return pl.ds(pl.multiple_of(value * 16, 16), 16)
 
     own_slots = pl.ds(pl.multiple_of(c * 2 * SLOTS, 2 * SLOTS), 2 * SLOTS)
     edges[D:WIDE, own_slots] = jnp.zeros((WIDE - D, 2 * SLOTS), BF16)
-    table[zh, x, c] = jnp.zeros((ROWS, WIDE), BF16)
+    wide[...] = jnp.zeros(wide.shape, F32)
     for copy in loads[:2]:
         copy.wait()
-    table[zh, x, c, 0:OWN, 0:D] = rel_ref[...].astype(BF16)
+    wide[0:OWN, 0:D] = rel_ref[...]
+    table[zh, x, c] = wide[0:ROWS, :].astype(BF16)
+    last_row = [wide[ROWS:OWN, LANE * i : LANE * i + LANE] for i in range(4)]
+    left[zh, x, c] = jnp.concatenate(
+        [fold(wide[0:ROWS, MAIN:WIDE]), *last_row, jnp.zeros((4, LANE), F32)], axis=0
+    ).astype(BF16)
     kinds[c] = jnp.concatenate([kind_ref[0], jnp.zeros((6, SLOTS), I32)], axis=0)
 
     pl.semaphore_wait(barrier, len(greet))
 
-    mine = table.at[zh, x, c]
-    quarter = table.at[zh, x, c, :, lane(y)]
-    to_zh = {k: send(quarter, quarter, zhs[k]) for k in ks}
-    own_x = [send(mine, mine, xs[k]) for k in ks]
+    mine, mine_left = table.at[zh, x, c, :, 0:MAIN], left.at[zh, x, c]
+    quarter = table.at[zh, x, c, rows(y), 0:MAIN]
+    to_zh = {k: [send(quarter, quarter, zhs[k]), send(mine_left, mine_left, zhs[k])] for k in (1, 3)}
+    own_x = [send(mine, mine, xs[k]) for k in ks] + [send(mine_left, mine_left, xs[k]) for k in ks]
     kinds_sib = send(kinds.at[c], kinds.at[c], sibling)
 
     both = jnp.concatenate([kind_ref[0, 0:1, :], kind_ref[0, 1:2, :]], axis=1)
-    shard_of = (both * 64528) >> 22
-    spot = both + (ROWS - OWN) * shard_of
+    shard_of, row_of = place_of(both)
+    spot = jnp.where(row_of < ROWS, ROWS * shard_of + row_of, -1)
+    hot_spare[...] = hot(jnp.where(row_of == ROWS, shard_of, -1), 0, 32)
 
     def fill(i, _):
         hot_all[i // 8, pl.ds(pl.multiple_of((i % 8) * ROWS, ROWS), ROWS), :] = hot(spot, i * ROWS, ROWS)
@@ -148,70 +172,84 @@
     for copy in loads[2:]:
         copy.wait()
 
-    def spread_y_first(k, lo, hi):
-        other = flip(zh, k)
-        piece = table.at[other, x, c, lo:hi, lane(y)]
+    def piece_of(k, lo, hi):
+        return table.at[flip(zh, k), x, c, rows(y), lo:hi]
+
+    def y_second(k, lo, hi):
+        piece = table.at[flip(zh, k), :, c, rows(y), lo:hi]
         return [send(piece, piece, ys[j]) for j in ks]
 
-    def spread_y_second(k, lo, hi):
-        other = flip(zh, k)
-        piece = table.at[other, :, c, lo:hi, lane(y)]
-        return [send(piece, piece, ys[j]) for j in ks]
-
-    def spread_x_first(k, lo, hi):
-        other = flip(zh, k)
-        piece = table.at[other, x, c, lo:hi, lane(y)]
+    def x_second(k, lo, hi):
+        piece = table.at[flip(zh, k), x, c, :, lo:hi]
         return [send(piece, piece, xs[j]) for j in ks]
 
-    def spread_x_second(k, lo, hi):
-        other = flip(zh, k)
-        piece = table.at[other, x, c, lo:hi, :]
-        return [send(piece, piece, xs[j]) for j in ks]
+    def spread(piece, targets):
+        return [send(piece, piece, targets[j]) for j in ks]
+
+    def left_of(k):
+        return left.at[flip(zh, k), x, c]
 
     def to_sibling(where):
-        piece = table.at[where, :, c]
-        return send(piece, piece, sibling)
+        piece, piece_left = table.at[where, :, c, :, 0:MAIN], left.at[where, :, c]
+        return [send(piece, piece, sibling), send(piece_left, piece_left, sibling)]
 
     def look_up(where, first):
+        folded = left[where].astype(F32).reshape(8, 16, LANE)
+        table[where, :, :, :, MAIN:WIDE] = unfold(folded[:, 0:8], 8).astype(BF16).reshape(4, 2, ROWS, LANE)
+        for shard in range(8):
+            for i in range(4):
+                spare[where, shard : shard + 1, LANE * i : LANE * i + LANE] = folded[shard, 8 + i : 9 + i]
         got = dot(table[where].reshape(8 * ROWS, WIDE)[:, 0:D], hot_all[where], 0, 0)
         if first:
             rr_buf[...] = got
         else:
             rr_buf[...] += got
 
-    cut = 48
-    arrived([to_zh[1]])
-    one_a = spread_y_first(1, 0, ROWS)
-    arrived([to_zh[3]])
-    three_a = spread_x_first(3, 0, ROWS)
+    cut = 256
+    arrived(to_zh[1])
+    one_a = spread(piece_of(1, 0, MAIN), ys)
+    one_left = spread(left_of(1), xs)
+    piece = piece_of(1, 0, cut)
+    relay_x = [send(piece, piece, zhs[3])]
+    arrived(to_zh[3])
+    three_a = spread(piece_of(3, 0, MAIN), xs)
+    three_left = spread(left_of(3), xs)
+    piece = piece_of(3, cut, MAIN)
+    relay_y = [send(piece, piece, zhs[1]), send(left_of(3), left_of(3), zhs[1])]
     arrived(own_x)
     sib_own = to_sibling(zh)
-    arrived([to_zh[2]])
-    two_x = spread_x_first(2, 0, cut)
-    two_y = spread_y_first(2, cut, ROWS)
+    arrived(relay_x)
+    two_x = spread(piece_of(2, 0, cut), xs)
+    arrived(relay_y)
+    two_y = spread(piece_of(2, cut, MAIN), ys)
+    two_left = spread(left_of(2), xs)
     arrived(one_a)
-    one_b = spread_x_second(1, 0, ROWS)
+    one_b = x_second(1, 0, MAIN)
     arrived(three_a)
-    three_b = spread_y_second(3, 0, ROWS)
-    arrived([sib_own])
+    three_b = y_second(3, 0, MAIN)
+    arrived(sib_own)
     look_up(zh, True)
     arrived(two_x)
-    two_xb = spread_y_second(2, 0, cut)
+    two_xb = y_second(2, 0, cut)
     arrived(two_y)
-    two_yb = spread_x_second(2, cut, ROWS)
+    two_yb = x_second(2, cut, MAIN)
+    arrived(one_left)
     arrived(one_b)
     sib_one = to_sibling(flip(zh, 1))
+    arrived(three_left)
     arrived(three_b)
     sib_three = to_sibling(flip(zh, 3))
-    arrived([sib_one])
+    arrived(sib_one)
     look_up(flip(zh, 1), False)
+    arrived(two_left)
     arrived(two_xb)
     arrived(two_yb)
     sib_two = to_sibling(flip(zh, 2))
-    arrived([sib_three])
+    arrived(sib_three)
     look_up(flip(zh, 3), False)
-    arrived([sib_two])
+    arrived(sib_two)
     look_up(flip(zh, 2), False)
+    rr_buf[...] += dot(spare[...].reshape(32, WIDE)[:, 0:D].astype(BF16), hot_spare[...], 0, 0)
 
     def front(turn, lhs):
         src = hot(src_ref[0, turn : turn + 1, :], 0, EP)
@@ -279,10 +317,13 @@
     for core in range(2):
         for turn in range(2):
             kind = kinds[core, turn : turn + 1, :]
-            shard = (kind * 64528) >> 22
+            shard, row = place_of(kind)
             half = shard >> 1
-            local = jnp.where(shard - 2 * half == c, kind - OWN * shard + ROWS * half, -1)
+            ours = shard - 2 * half == c
+            local = jnp.where(ours & (row < ROWS), ROWS * half + row, -1)
             at = (core * 2 + turn) * SLOTS
+
+            hot_mine_spare[:, at : at + SLOTS] = hot(jnp.where(ours & (row == ROWS), half, -1), 0, 16)
 
             def fill_mine(i, _, local=local, at=at):
                 hot_mine[i // 4, pl.ds(pl.multiple_of((i % 4) * ROWS, ROWS), ROWS), at : at + SLOTS] = hot(
@@ -297,9 +338,17 @@
     edges_sib.append(back(1, rhs_in[...]))
     arrived(edges_sib)
 
+    last_rows = dot(hot_mine_spare[...], edges[...], 1, 1)
+
     def chunk(i):
         got = dot(hot_mine[i], edges[...], 1, 1)
-        part[i] = got.astype(BF16).reshape(4, ROWS, WIDE)
+        part[i] = got[:, 0:MAIN].astype(BF16).reshape(4, ROWS, MAIN)
+        for j in range(4):
+            at = 4 * i + j
+            spare_rows = [last_rows[at : at + 1, LANE * q : LANE * q + LANE] for q in range(4)]
+            part_left[i, j] = jnp.concatenate(
+                [fold(got[ROWS * j : ROWS * j + ROWS, MAIN:WIDE]), *spare_rows, jnp.zeros((4, LANE), F32)], axis=0
+            ).astype(BF16)
 
     def x_first(i):
         chunk(i)
@@ -307,9 +356,10 @@
 
     def y_first(i):
         chunk(i)
-        return {k: send(part.at[i, :, :, lane(flip(y, k))], y_in.at[i - 2, k - 1], ys[k]) for k in ks}
+        return {k: send(part.at[i, :, rows(flip(y, k))], y_in.at[i - 2, k - 1], ys[k]) for k in ks}
 
     first = {0: x_first(0), 2: y_first(2), 1: x_first(1), 3: y_first(3)}
+    first_left = {k: send(part_left.at[:, flip(x, k)], l_in.at[k - 1], xs[k]) for k in ks}
 
     new_rhs, new_rst = adagrad(rhs_in[...], rst_in[0:1, :], rhs_grad())
     rhs_out[...] = new_rhs
@@ -326,11 +376,11 @@
         for k in ks:
             total += x_in[i, k - 1].astype(F32)
         stage2y[i] = total.astype(BF16)
-        return {k: send(stage2y.at[i, :, lane(flip(y, k))], y2_in.at[i, k - 1], ys[k]) for k in ks}
+        return {k: send(stage2y.at[i, rows(flip(y, k))], y2_in.at[i, k - 1], ys[k]) for k in ks}
 
     def y_then_x(i):
         arrived(first[i].values())
-        total = part[i, :, :, lane(y)].astype(F32)
+        total = part[i, :, rows(y)].astype(F32)
         for k in ks:
             total += y_in[i - 2, k - 1].astype(F32)
         stage2x[i - 2] = total.astype(BF16)
@@ -338,12 +388,22 @@
 
     second = {0: x_then_y(0), 2: y_then_x(2), 1: x_then_y(1), 3: y_then_x(3)}
 
+    arrived(first_left.values())
+    sum_left = part_left[:, x].astype(F32)
+    for k in ks:
+        sum_left += l_in[k - 1].astype(F32)
+    l_y[y] = sum_left.astype(BF16)
+    second_left = [send(l_y.at[y], l_y.at[y], ys[k]) for k in ks]
+
     for i in (0, 2, 1, 3):
         arrived(second[i].values())
-        total = (stage2y[i, :, lane(y)] if i < 2 else stage2x[i - 2, x]).astype(F32)
+        total = (stage2y[i, rows(y)] if i < 2 else stage2x[i - 2, x]).astype(F32)
         for k in ks:
             total += (y2_in[i, k - 1] if i < 2 else x2_in[i - 2, k - 1]).astype(F32)
-        z_out[i] = total.astype(BF16)
+        z_out[i, :, 0:MAIN] = total.astype(BF16)
+    arrived(second_left)
+    all_left = (l_y[0].astype(F32) + l_y[1].astype(F32)) + (l_y[2].astype(F32) + l_y[3].astype(F32))
+    z_out[:, :, MAIN:WIDE] = all_left.astype(BF16)
 
     za = {k: send(z_out.at[flip(zh, k)], z_in.at[k - 1], zhs[k]) for k in ks}
     arrived(za.values())
@@ -354,11 +414,15 @@
     zb = [send(low.at[zl], low.at[zl], zls[k]) for k in ks]
     arrived(zb)
     both_z = (low[0].astype(F32) + low[1].astype(F32)) + (low[2].astype(F32) + low[3].astype(F32))
-    full[:, lane(y)] = both_z
-    last = [send(full.at[:, lane(y)], full.at[:, lane(y)], ys[k]) for k in ks]
+    full[rows(y), 0:MAIN] = both_z[:, 0:MAIN]
+    last = [send(full.at[rows(y), 0:MAIN], full.at[rows(y), 0:MAIN], ys[k]) for k in ks]
+    wide[0:ROWS, MAIN:WIDE] = unfold(both_z[0:8, MAIN:WIDE].reshape(1, 8, LANE), 1)[0]
+    for i in range(4):
+        wide[ROWS:OWN, LANE * i : LANE * i + LANE] = both_z[8 + i : 9 + i, MAIN:WIDE]
     arrived(last)
-
-    total = full[0:OWN, 0:D]
+    wide[0:ROWS, 0:MAIN] = full[...]
+
+    total = wide[0:OWN, 0:D]
     eye = lax.broadcasted_iota(I32, (OWN, OWN), 0) == lax.broadcasted_iota(I32, (OWN, OWN), 1)
     old = jnp.sum(jnp.where(eye, relst_ref[...], 0.0), axis=1, keepdims=True)
     new = old + jnp.sum(total * total, axis=1, keepdims=True) / D
@@ -386,7 +450,7 @@
         copy.wait()
 
 
-N_COPIES = 96
+N_COPIES = 112
 
 
 def body(
@@ -411,9 +475,14 @@
             *[pltpu.VMEM((1, 2, SLOTS), I32) for _ in range(4)],
             *[pltpu.VMEM(out.shape, out.dtype) for out in out_shape],
             pltpu.VMEM((4, 4, 2, ROWS, WIDE), BF16),
+            pltpu.VMEM((4, 4, 2, 16, LANE), BF16),
+            pltpu.VMEM((4, 8, WIDE), F32),
             pltpu.VMEM((4, 8 * ROWS, 2 * SLOTS), BF16),
+            pltpu.VMEM((32, 2 * SLOTS), BF16),
             pltpu.VMEM((4, 4 * ROWS, 4 * SLOTS), BF16),
+            pltpu.VMEM((16, 4 * SLOTS), BF16),
             pltpu.VMEM((2, 8, SLOTS), I32),
+            pltpu.VMEM((72, WIDE), F32),
             pltpu.VMEM((D, SLOTS), F32),
             pltpu.VMEM((D, 2 * SLOTS), F32),
             pltpu.VMEM((D, SLOTS), BF16),
@@ -424,17 +493,20 @@
             pltpu.VMEM((8, EP), F32),
             pltpu.VMEM((D, EP), BF16),
             pltpu.VMEM((8, EP), F32),
-            pltpu.VMEM((4, 4, ROWS, WIDE), BF16),
-            pltpu.VMEM((2, 3, ROWS, WIDE), BF16),
-            pltpu.VMEM((2, 3, 4, ROWS, LANE), BF16),
-            pltpu.VMEM((2, 3, ROWS, LANE), BF16),
-            pltpu.VMEM((2, 3, ROWS, LANE), BF16),
-            pltpu.VMEM((4, ROWS, LANE), BF16),
-            pltpu.VMEM((3, ROWS, LANE), BF16),
-            pltpu.VMEM((4, ROWS, LANE), BF16),
-            pltpu.VMEM((ROWS, WIDE), F32),
-            pltpu.VMEM((2, 4, ROWS, LANE), BF16),
-            pltpu.VMEM((2, ROWS, WIDE), BF16),
+            pltpu.VMEM((4, 4, ROWS, MAIN), BF16),
+            pltpu.VMEM((4, 4, 16, LANE), BF16),
+            pltpu.VMEM((3, 4, 16, LANE), BF16),
+            pltpu.VMEM((4, 4, 16, LANE), BF16),
+            pltpu.VMEM((2, 3, ROWS, MAIN), BF16),
+            pltpu.VMEM((2, 3, 4, 16, MAIN), BF16),
+            pltpu.VMEM((2, 3, 16, MAIN), BF16),
+            pltpu.VMEM((2, 3, 16, MAIN), BF16),
+            pltpu.VMEM((4, 16, WIDE), BF16),
+            pltpu.VMEM((3, 16, WIDE), BF16),
+            pltpu.VMEM((4, 16, WIDE), BF16),
+            pltpu.VMEM((ROWS, MAIN), F32),
+            pltpu.VMEM((2, 4, 16, MAIN), BF16),
+            pltpu.VMEM((2, ROWS, MAIN), BF16),
             pltpu.SemaphoreType.DMA((N_COPIES,)),
             pltpu.SemaphoreType.DMA((N_COPIES,)),
             pltpu.SemaphoreType.DMA((10,)),

time: 82.2 us -> 78.9 us (0.960)
  Pallas kernels: 80.9 us -> 78 us
    pallas_call x1, Pallas kernels: 79.1 us -> 76.2 us  [body(): pl.pallas_call(kernel, out_shape=out_shape, in_specs=[hbm] * 10 + [smem],...]
where the time goes in v4:
time: 78.9 us; the launch traced here: 78.7 us
  Pallas kernels  78 us (99%)
    pallas_call x1, Pallas kernels, body(): pl.pallas_call(kernel, out_shape=out_shape, in_specs=[hbm] * 10 + [smem],...  76.2 us
    pallas_call x1, Pallas kernels, body(): pl.pallas_call(hand_on, out_shape=out_shape, in_specs=[hbm] * 6, out_spec...  1.79 us

profile of v4, /device:TPU:1, one launch (start us, length us, event | category | flops | bytes accessed | tf_op | source)
XLA Modules:
  0.0 78.7 jit_solution(15935832321844041507)
XLA Ops:
  0.6 76.2 %train.1 = (bf16[400,128]{1,0:T(8,128)(2,1)}, f32[1,128]{1,0:T(1,128)}, bf16[400,128]{1,0:T(8,128)(2,1)}, f32[1,128]{1,0:T(1,128)}, f32[65,400]{1,0:T(8,128)}, /*index=5*/f32[1,65]{1,0:T(1,128)}) custom-call(bf16[400,128]{1,0:T(8,128)(2,1)} %bitcast.10, f32[1,128]{1,0:T(1,128)} %bitcast.12, bf16[400,128]{1,0:T(8,128)(2,1)} %bitcast.11, f32[1,128]{1,0:T(1,128)} %bitcast.13, ...), custom_call_target="tpu_custom_call" | custom-call | tf_op jit(solution)/shard_map/train/pallas_call | solution.py:467
  76.9 1.8 %hand_on.1 = (bf16[400,128]{1,0:T(8,128)(2,1)}, f32[1,128]{1,0:T(1,128)}, bf16[400,128]{1,0:T(8,128)(2,1)}, f32[1,128]{1,0:T(1,128)}, f32[65,400]{1,0:T(8,128)}, /*index=5*/f32[1,65]{1,0:T(1,128)}) custom-call(bf16[400,128]{1,0:T(8,128)(2,1)} %get-tuple-element.18.refs_0_, f32[1,128]{1,0:T(1,128)} %get-tuple-element.19.refs_1_, ...), custom_call_target="tpu_custom_call" | custom-call | tf_op jit(solution)/shard_map/hand_on/pallas_call | solution.py:523

commit v5 on v4

--- a/solution.py
+++ b/solution.py
@@ -74,7 +74,7 @@
     lhs_res, lst_res, rhs_res, rst_res, rel_res, relst_res,
     lhs_ref, lst_ref, rhs_ref, rst_ref, rel_ref, relst_ref, src_ref, dst_ref, kind_ref, neg_ref,
     lhs_out, lst_out, rhs_out, rst_out, rel_out, relst_out,
-    table, left, spare, hot_all, hot_spare, hot_mine, hot_mine_spare, kinds, wide, a_buf, rr_buf, q_buf, m_hi, m_lo, edges,
+    times_buf, row_sums, table, left, spare, hot_all, hot_spare, hot_mine, hot_mine_spare, kinds, wide, a_buf, rr_buf, q_buf, m_hi, m_lo, edges,
     rhs_send, rst_send, rhs_in, rst_in, part, part_left, l_in, l_y, x_in, y_in, x2_in, y2_in, z_out, z_in, low, full, stage2x, stage2y,
     send_sem, recv_sem, in_sem, out_sem,
 ):
@@ -112,7 +112,7 @@
             )
         )
     ]
-    for copy in loads:
+    for copy in loads[:2]:
         copy.start()
     started, stores = [], []
 
@@ -138,8 +138,11 @@
     def rows(value):
         return pl.ds(pl.multiple_of(value * 16, 16), 16)
 
-    own_slots = pl.ds(pl.multiple_of(c * 2 * SLOTS, 2 * SLOTS), 2 * SLOTS)
-    edges[D:WIDE, own_slots] = jnp.zeros((WIDE - D, 2 * SLOTS), BF16)
+    def slot(turn):
+        return pl.ds(pl.multiple_of((turn * 2 + c) * SLOTS, SLOTS), SLOTS)
+
+    for turn in range(2):
+        edges[D:WIDE, slot(turn)] = jnp.zeros((WIDE - D, SLOTS), BF16)
     wide[...] = jnp.zeros(wide.shape, F32)
     for copy in loads[:2]:
         copy.wait()
@@ -158,6 +161,9 @@
     to_zh = {k: [send(quarter, quarter, zhs[k]), send(mine_left, mine_left, zhs[k])] for k in (1, 3)}
     own_x = [send(mine, mine, xs[k]) for k in ks] + [send(mine_left, mine_left, xs[k]) for k in ks]
     kinds_sib = send(kinds.at[c], kinds.at[c], sibling)
+
+    for copy in loads[2:]:
+        copy.start()
 
     both = jnp.concatenate([kind_ref[0, 0:1, :], kind_ref[0, 1:2, :]], axis=1)
     shard_of, row_of = place_of(both)
@@ -205,28 +211,35 @@
         else:
             rr_buf[...] += got
 
+    def source_rows(turn, lhs):
+        a_buf[...] = dot(lhs, hot(src_ref[0, turn : turn + 1, :], 0, EP), 1, 0)
+
     cut = 256
     arrived(to_zh[1])
-    one_a = spread(piece_of(1, 0, MAIN), ys)
-    one_left = spread(left_of(1), xs)
     piece = piece_of(1, 0, cut)
     relay_x = [send(piece, piece, zhs[3])]
+    one_a = spread(piece_of(1, 0, MAIN), ys)
     arrived(to_zh[3])
-    three_a = spread(piece_of(3, 0, MAIN), xs)
-    three_left = spread(left_of(3), xs)
     piece = piece_of(3, cut, MAIN)
     relay_y = [send(piece, piece, zhs[1]), send(left_of(3), left_of(3), zhs[1])]
+    three_a = spread(piece_of(3, 0, MAIN), xs)
+    one_left = spread(left_of(1), xs)
+    three_left = spread(left_of(3), xs)
     arrived(own_x)
     sib_own = to_sibling(zh)
+    arrived(one_a)
+    one_b = x_second(1, 0, MAIN)
+    arrived(three_a)
+    three_b = y_second(3, 0, MAIN)
     arrived(relay_x)
     two_x = spread(piece_of(2, 0, cut), xs)
     arrived(relay_y)
     two_y = spread(piece_of(2, cut, MAIN), ys)
     two_left = spread(left_of(2), xs)
-    arrived(one_a)
-    one_b = x_second(1, 0, MAIN)
-    arrived(three_a)
-    three_b = y_second(3, 0, MAIN)
+    source_rows(0, lhs_ref[...])
+    for turn in range(2):
+        drawn = hot(neg_ref[0, turn : turn + 1, :], 0, EP)
+        times_buf[turn] = jnp.broadcast_to(jnp.sum(drawn.astype(F32), axis=1, keepdims=True), (EP, LANE))
     arrived(sib_own)
     look_up(zh, True)
     arrived(two_x)
@@ -251,9 +264,7 @@
     look_up(flip(zh, 2), False)
     rr_buf[...] += dot(spare[...].reshape(32, WIDE)[:, 0:D].astype(BF16), hot_spare[...], 0, 0)
 
-    def front(turn, lhs):
-        src = hot(src_ref[0, turn : turn + 1, :], 0, EP)
-        a_buf[...] = dot(lhs, src, 1, 0)
+    def front(turn):
         cols = slice(turn * SLOTS, (turn + 1) * SLOTS)
         a_re, a_im = a_buf[0:HALF, :], a_buf[HALF:D, :]
         r_re, r_im = rr_buf[0:HALF, cols], rr_buf[HALF:D, cols]
@@ -263,8 +274,7 @@
         score = dot(rhs, q_buf[...], 0, 0)
         dst = dst_ref[0, turn : turn + 1, :]
         is_dst = lax.broadcasted_iota(I32, (EP, SLOTS), 0) == dst
-        drawn = hot(neg_ref[0, turn : turn + 1, :], 0, EP)
-        times = jnp.sum(drawn.astype(F32), axis=1, keepdims=True)
+        times = times_buf[turn, :, 0:1]
         pos = jnp.sum(jnp.where(is_dst, score, 0.0), axis=0, keepdims=True)
         live = jnp.where(
             lax.broadcasted_iota(I32, (1, SLOTS), 1) < count_ref[0, turn], 1.0, 0.0
@@ -290,17 +300,17 @@
         a_re, a_im = a_buf[0:HALF, :], a_buf[HALF:D, :]
         r_re, r_im = rr_buf[0:HALF, cols], rr_buf[HALF:D, cols]
         grad_r = jnp.concatenate([d_re * a_re + d_im * a_im, d_im * a_re - d_re * a_im], axis=0)
+        edges[0:D, slot(turn)] = grad_r.astype(BF16)
+        copy = send(edges.at[:, slot(turn)], edges.at[:, slot(turn)], sibling)
         a_buf[...] = jnp.concatenate([d_re * r_re + d_im * r_im, d_im * r_re - d_re * r_im], axis=0)
-        spot_ = pl.ds(pl.multiple_of((c * 2 + turn) * SLOTS, SLOTS), SLOTS)
-        edges[0:D, spot_] = grad_r.astype(BF16)
-        return send(edges.at[:, spot_], edges.at[:, spot_], sibling)
+        return copy
 
     def lhs_grad(turn):
         src = hot(src_ref[0, turn : turn + 1, :], 0, EP)
         high, rest = split(a_buf[...])
         return dot(high, src, 1, 1) + dot(rest, src, 1, 1)
 
-    front(0, lhs_ref[...])
+    front(0)
     weights(0, rhs_ref[...])
     new_rhs, new_rst = adagrad(rhs_ref[...], rst_ref[...], rhs_grad())
     rhs_send[...] = new_rhs
@@ -311,7 +321,8 @@
     lhs_out[...] = new_lhs
     lst_out[...] = new_lst
 
-    front(1, lhs_out[...])
+    source_rows(1, lhs_out[...])
+    front(1)
 
     arrived([kinds_sib])
     for core in range(2):
@@ -321,7 +332,7 @@
             half = shard >> 1
             ours = shard - 2 * half == c
             local = jnp.where(ours & (row < ROWS), ROWS * half + row, -1)
-            at = (core * 2 + turn) * SLOTS
+            at = (turn * 2 + core) * SLOTS
 
             hot_mine_spare[:, at : at + SLOTS] = hot(jnp.where(ours & (row == ROWS), half, -1), 0, 16)
 
@@ -333,15 +344,20 @@
 
             lax.fori_loop(0, 16, fill_mine, 0)
 
+    arrived(edges_sib)
+    early, late = slice(0, 2 * SLOTS), slice(2 * SLOTS, 4 * SLOTS)
+    for i in range(4):
+        row_sums[i] = dot(hot_mine[i, :, early], edges[:, early], 1, 1)
+    row_sums[4, 0:16] = dot(hot_mine_spare[:, early], edges[:, early], 1, 1)
+
     arrived(passed)
     weights(1, rhs_in[...])
-    edges_sib.append(back(1, rhs_in[...]))
-    arrived(edges_sib)
-
-    last_rows = dot(hot_mine_spare[...], edges[...], 1, 1)
+    arrived([back(1, rhs_in[...])])
+
+    last_rows = row_sums[4, 0:16] + dot(hot_mine_spare[:, late], edges[:, late], 1, 1)
 
     def chunk(i):
-        got = dot(hot_mine[i], edges[...], 1, 1)
+        got = row_sums[i] + dot(hot_mine[i, :, late], edges[:, late], 1, 1)
         part[i] = got[:, 0:MAIN].astype(BF16).reshape(4, ROWS, MAIN)
         for j in range(4):
             at = 4 * i + j
@@ -474,6 +490,8 @@
             pltpu.VMEM((OWN, D), F32), pltpu.VMEM((1, OWN), F32),
             *[pltpu.VMEM((1, 2, SLOTS), I32) for _ in range(4)],
             *[pltpu.VMEM(out.shape, out.dtype) for out in out_shape],
+            pltpu.VMEM((2, EP, LANE), F32),
+            pltpu.VMEM((5, 4 * ROWS, WIDE), F32),
             pltpu.VMEM((4, 4, 2, ROWS, WIDE), BF16),
             pltpu.VMEM((4, 4, 2, 16, LANE), BF16),
             pltpu.VMEM((4, 8, WIDE), F32),

time: 78.9 us -> 77.1 us (0.977)
  Pallas kernels: 78 us -> 75.7 us
    pallas_call x1, Pallas kernels: 76.2 us -> 73.9 us  [body(): pl.pallas_call(kernel, out_shape=out_shape, in_specs=[hbm] * 10 + [smem],...]
where the time goes in v5:
time: 77.1 us; the launch traced here: 76.3 us
  Pallas kernels  75.7 us (98%)
    pallas_call x1, Pallas kernels, body(): pl.pallas_call(kernel, out_shape=out_shape, in_specs=[hbm] * 10 + [smem],...  73.9 us
    pallas_call x1, Pallas kernels, body(): pl.pallas_call(hand_on, out_shape=out_shape, in_specs=[hbm] * 6, out_spec...  1.79 us

profile of v5, /device:TPU:1, one launch (start us, length us, event | category | flops | bytes accessed | tf_op | source)
XLA Modules:
  0.0 76.3 jit_solution(5396341737969650940)
XLA Ops:
  0.6 73.9 %train.1 = (bf16[400,128]{1,0:T(8,128)(2,1)}, f32[1,128]{1,0:T(1,128)}, bf16[400,128]{1,0:T(8,128)(2,1)}, f32[1,128]{1,0:T(1,128)}, f32[65,400]{1,0:T(8,128)}, /*index=5*/f32[1,65]{1,0:T(1,128)}) custom-call(bf16[400,128]{1,0:T(8,128)(2,1)} %bitcast.10, f32[1,128]{1,0:T(1,128)} %bitcast.12, bf16[400,128]{1,0:T(8,128)(2,1)} %bitcast.11, f32[1,128]{1,0:T(1,128)} %bitcast.13, ...), custom_call_target="tpu_custom_call" | custom-call | tf_op jit(solution)/shard_map/train/pallas_call | solution.py:483
  74.5 1.8 %hand_on.1 = (bf16[400,128]{1,0:T(8,128)(2,1)}, f32[1,128]{1,0:T(1,128)}, bf16[400,128]{1,0:T(8,128)(2,1)}, f32[1,128]{1,0:T(1,128)}, f32[65,400]{1,0:T(8,128)}, /*index=5*/f32[1,65]{1,0:T(1,128)}) custom-call(bf16[400,128]{1,0:T(8,128)(2,1)} %get-tuple-element.18.refs_0_, f32[1,128]{1,0:T(1,128)} %get-tuple-element.19.refs_1_, ...), custom_call_target="tpu_custom_call" | custom-call | tf_op jit(solution)/shard_map/hand_on/pallas_call | solution.py:541

commit v6 on v5

--- a/solution.py
+++ b/solution.py
@@ -70,12 +70,12 @@
 
 
 def kernel(
-    lhs_hbm, lst_hbm, rhs_hbm, rst_hbm, rel_hbm, relst_hbm, src_hbm, dst_hbm, kind_hbm, neg_hbm, count_ref,
+    lhs_hbm, lst_hbm, rhs_hbm, rst_hbm, rel_hbm, relst_hbm, src_hbm, dst_hbm, kind_hbm, neg_hbm, count_hbm,
     lhs_res, lst_res, rhs_res, rst_res, rel_res, relst_res,
-    lhs_ref, lst_ref, rhs_ref, rst_ref, rel_ref, relst_ref, src_ref, dst_ref, kind_ref, neg_ref,
+    lhs_ref, lst_ref, rhs_ref, rst_ref, rel_ref, relst_ref, src_ref, dst_ref, kind_ref, neg_ref, count_ref,
     lhs_out, lst_out, rhs_out, rst_out, rel_out, relst_out,
     times_buf, row_sums, table, left, spare, hot_all, hot_spare, hot_mine, hot_mine_spare, kinds, wide, a_buf, rr_buf, q_buf, m_hi, m_lo, edges,
-    rhs_send, rst_send, rhs_in, rst_in, part, part_left, l_in, l_y, x_in, y_in, x2_in, y2_in, z_out, z_in, low, full, stage2x, stage2y,
+    rhs_send, rst_send, rhs_in, rst_in, part, part_left, l_in, l_y, x_in, y_in, x2_in, y2_in, z_out, z_in, low, stage2x, stage2y,
     send_sem, recv_sem, in_sem, out_sem,
 ):
     grp, dev = lax.axis_index("grp"), lax.axis_index("dev")
@@ -109,6 +109,7 @@
             (
                 (rel_hbm, rel_ref), (kind_hbm, kind_ref), (lhs_hbm, lhs_ref), (src_hbm, src_ref), (rhs_hbm, rhs_ref),
                 (dst_hbm, dst_ref), (neg_hbm, neg_ref), (lst_hbm, lst_ref), (rst_hbm, rst_ref), (relst_hbm, relst_ref),
+                (count_hbm, count_ref),
             )
         )
     ]
@@ -141,8 +142,7 @@
     def slot(turn):
         return pl.ds(pl.multiple_of((turn * 2 + c) * SLOTS, SLOTS), SLOTS)
 
-    for turn in range(2):
-        edges[D:WIDE, slot(turn)] = jnp.zeros((WIDE - D, SLOTS), BF16)
+    edges[D:WIDE, :] = jnp.zeros((WIDE - D, 4 * SLOTS), BF16)
     wide[...] = jnp.zeros(wide.shape, F32)
     for copy in loads[:2]:
         copy.wait()
@@ -232,20 +232,16 @@
     arrived(three_a)
     three_b = y_second(3, 0, MAIN)
     arrived(relay_x)
-    two_x = spread(piece_of(2, 0, cut), xs)
     arrived(relay_y)
-    two_y = spread(piece_of(2, cut, MAIN), ys)
-    two_left = spread(left_of(2), xs)
+    piece = piece_of(2, 0, MAIN)
+    two = [send(piece, piece, place(x_=flip(x, i), y_=flip(y, j))) for i in ks for j in ks]
+    two += spread(piece, xs) + spread(piece, ys) + spread(left_of(2), xs)
     source_rows(0, lhs_ref[...])
     for turn in range(2):
         drawn = hot(neg_ref[0, turn : turn + 1, :], 0, EP)
         times_buf[turn] = jnp.broadcast_to(jnp.sum(drawn.astype(F32), axis=1, keepdims=True), (EP, LANE))
     arrived(sib_own)
     look_up(zh, True)
-    arrived(two_x)
-    two_xb = y_second(2, 0, cut)
-    arrived(two_y)
-    two_yb = x_second(2, cut, MAIN)
     arrived(one_left)
     arrived(one_b)
     sib_one = to_sibling(flip(zh, 1))
@@ -254,9 +250,7 @@
     sib_three = to_sibling(flip(zh, 3))
     arrived(sib_one)
     look_up(flip(zh, 1), False)
-    arrived(two_left)
-    arrived(two_xb)
-    arrived(two_yb)
+    arrived(two)
     sib_two = to_sibling(flip(zh, 2))
     arrived(sib_three)
     look_up(flip(zh, 3), False)
@@ -277,7 +271,7 @@
         times = times_buf[turn, :, 0:1]
         pos = jnp.sum(jnp.where(is_dst, score, 0.0), axis=0, keepdims=True)
         live = jnp.where(
-            lax.broadcasted_iota(I32, (1, SLOTS), 1) < count_ref[0, turn], 1.0, 0.0
+            lax.broadcasted_iota(I32, (1, SLOTS), 1) < count_ref[0:1, turn : turn + 1], 1.0, 0.0
         )
         neg_exp = jnp.exp(score)
         pos_exp = jnp.exp(pos)
@@ -301,7 +295,7 @@
         r_re, r_im = rr_buf[0:HALF, cols], rr_buf[HALF:D, cols]
         grad_r = jnp.concatenate([d_re * a_re + d_im * a_im, d_im * a_re - d_re * a_im], axis=0)
         edges[0:D, slot(turn)] = grad_r.astype(BF16)
-        copy = send(edges.at[:, slot(turn)], edges.at[:, slot(turn)], sibling)
+        copy = send(edges.at[0:D, slot(turn)], edges.at[0:D, slot(turn)], sibling)
         a_buf[...] = jnp.concatenate([d_re * r_re + d_im * r_im, d_im * r_re - d_re * r_im], axis=0)
         return copy
 
@@ -359,20 +353,27 @@
     def chunk(i):
         got = row_sums[i] + dot(hot_mine[i, :, late], edges[:, late], 1, 1)
         part[i] = got[:, 0:MAIN].astype(BF16).reshape(4, ROWS, MAIN)
+        return got[:, MAIN:WIDE]
+
+    def fold_chunk(i, tails):
         for j in range(4):
             at = 4 * i + j
             spare_rows = [last_rows[at : at + 1, LANE * q : LANE * q + LANE] for q in range(4)]
             part_left[i, j] = jnp.concatenate(
-                [fold(got[ROWS * j : ROWS * j + ROWS, MAIN:WIDE]), *spare_rows, jnp.zeros((4, LANE), F32)], axis=0
+                [fold(tails[ROWS * j : ROWS * j + ROWS]), *spare_rows, jnp.zeros((4, LANE), F32)], axis=0
             ).astype(BF16)
 
     def x_first(i):
-        chunk(i)
-        return {k: send(part.at[i, flip(x, k)], x_in.at[i, k - 1], xs[k]) for k in ks}
+        tails = chunk(i)
+        copies = {k: send(part.at[i, flip(x, k)], x_in.at[i, k - 1], xs[k]) for k in ks}
+        fold_chunk(i, tails)
+        return copies
 
     def y_first(i):
-        chunk(i)
-        return {k: send(part.at[i, :, rows(flip(y, k))], y_in.at[i - 2, k - 1], ys[k]) for k in ks}
+        tails = chunk(i)
+        copies = {k: send(part.at[i, :, rows(flip(y, k))], y_in.at[i - 2, k - 1], ys[k]) for k in ks}
+        fold_chunk(i, tails)
+        return copies
 
     first = {0: x_first(0), 2: y_first(2), 1: x_first(1), 3: y_first(3)}
     first_left = {k: send(part_left.at[:, flip(x, k)], l_in.at[k - 1], xs[k]) for k in ks}
@@ -430,13 +431,13 @@
     zb = [send(low.at[zl], low.at[zl], zls[k]) for k in ks]
     arrived(zb)
     both_z = (low[0].astype(F32) + low[1].astype(F32)) + (low[2].astype(F32) + low[3].astype(F32))
-    full[rows(y), 0:MAIN] = both_z[:, 0:MAIN]
-    last = [send(full.at[rows(y), 0:MAIN], full.at[rows(y), 0:MAIN], ys[k]) for k in ks]
+    own_rows = wide.at[rows(y), 0:MAIN]
+    own_rows[...] = both_z[:, 0:MAIN]
+    last = [send(own_rows, own_rows, ys[k]) for k in ks]
     wide[0:ROWS, MAIN:WIDE] = unfold(both_z[0:8, MAIN:WIDE].reshape(1, 8, LANE), 1)[0]
     for i in range(4):
         wide[ROWS:OWN, LANE * i : LANE * i + LANE] = both_z[8 + i : 9 + i, MAIN:WIDE]
     arrived(last)
-    wide[0:ROWS, 0:MAIN] = full[...]
 
     total = wide[0:OWN, 0:D]
     eye = lax.broadcasted_iota(I32, (OWN, OWN), 0) == lax.broadcasted_iota(I32, (OWN, OWN), 1)
@@ -474,7 +475,6 @@
     src_index, dst_index, rel_index, neg_index, edge_count,
 ):
     hbm = pl.BlockSpec(memory_space=pltpu.HBM)
-    smem = pl.BlockSpec(memory_space=pltpu.SMEM)
     shape = jax.ShapeDtypeStruct
     out_shape = (
         shape((D, EP), BF16), shape((1, EP), F32), shape((D, EP), BF16), shape((1, EP), F32),
@@ -483,12 +483,13 @@
     outs = pl.pallas_call(
         kernel,
         out_shape=out_shape,
-        in_specs=[hbm] * 10 + [smem],
+        in_specs=[hbm] * 11,
         out_specs=(hbm,) * 6,
         scratch_shapes=[
             pltpu.VMEM((D, EP), BF16), pltpu.VMEM((1, EP), F32), pltpu.VMEM((D, EP), BF16), pltpu.VMEM((1, EP), F32),
             pltpu.VMEM((OWN, D), F32), pltpu.VMEM((1, OWN), F32),
             *[pltpu.VMEM((1, 2, SLOTS), I32) for _ in range(4)],
+            pltpu.VMEM((1, 2), I32),
             *[pltpu.VMEM(out.shape, out.dtype) for out in out_shape],
             pltpu.VMEM((2, EP, LANE), F32),
             pltpu.VMEM((5, 4 * ROWS, WIDE), F32),
@@ -522,12 +523,11 @@
             pltpu.VMEM((4, 16, WIDE), BF16),
             pltpu.VMEM((3, 16, WIDE), BF16),
             pltpu.VMEM((4, 16, WIDE), BF16),
-            pltpu.VMEM((ROWS, MAIN), F32),
             pltpu.VMEM((2, 4, 16, MAIN), BF16),
             pltpu.VMEM((2, ROWS, MAIN), BF16),
             pltpu.SemaphoreType.DMA((N_COPIES,)),
             pltpu.SemaphoreType.DMA((N_COPIES,)),
-            pltpu.SemaphoreType.DMA((10,)),
+            pltpu.SemaphoreType.DMA((11,)),
             pltpu.SemaphoreType.DMA((6,)),
         ],
         compiler_params=pltpu.CompilerParams(

time: 77.1 us -> 74.7 us (0.969)
  Pallas kernels: 75.7 us -> 73 us
    pallas_call x1, Pallas kernels: 73.9 us -> 71.3 us  [body(): pl.pallas_call(kernel, out_shape=out_shape, in_specs=[hbm] * 11, out_spec...]
where the time goes in v6:
time: 74.7 us; the launch traced here: 73.7 us
  Pallas kernels  73 us (98%)
    pallas_call x1, Pallas kernels, body(): pl.pallas_call(kernel, out_shape=out_shape, in_specs=[hbm] * 11, out_spec...  71.3 us
    pallas_call x1, Pallas kernels, body(): pl.pallas_call(hand_on, out_shape=out_shape, in_specs=[hbm] * 6, out_spec...  1.79 us

profile of v6, /device:TPU:1, one launch (start us, length us, event | category | flops | bytes accessed | tf_op | source)
XLA Modules:
  0.0 73.7 jit_solution(6910065174208750893)
XLA Ops:
  0.6 71.3 %train.1 = (bf16[400,128]{1,0:T(8,128)(2,1)}, f32[1,128]{1,0:T(1,128)}, bf16[400,128]{1,0:T(8,128)(2,1)}, f32[1,128]{1,0:T(1,128)}, f32[65,400]{1,0:T(8,128)}, /*index=5*/f32[1,65]{1,0:T(1,128)}) custom-call(bf16[400,128]{1,0:T(8,128)(2,1)} %bitcast.10, f32[1,128]{1,0:T(1,128)} %bitcast.12, bf16[400,128]{1,0:T(8,128)(2,1)} %bitcast.11, f32[1,128]{1,0:T(1,128)} %bitcast.13, ...), custom_call_target="tpu_custom_call" | custom-call | tf_op jit(solution)/shard_map/train/pallas_call | solution.py:483
  71.9 1.8 %hand_on.1 = (bf16[400,128]{1,0:T(8,128)(2,1)}, f32[1,128]{1,0:T(1,128)}, bf16[400,128]{1,0:T(8,128)(2,1)}, f32[1,128]{1,0:T(1,128)}, f32[65,400]{1,0:T(8,128)}, /*index=5*/f32[1,65]{1,0:T(1,128)}) custom-call(bf16[400,128]{1,0:T(8,128)(2,1)} %get-tuple-element.18.refs_0_, f32[1,128]{1,0:T(1,128)} %get-tuple-element.19.refs_1_, ...), custom_call_target="tpu_custom_call" | custom-call | tf_op jit(solution)/shard_map/hand_on/pallas_call | solution.py:541

commit v7 on v6

--- a/solution.py
+++ b/solution.py
@@ -92,7 +92,7 @@
 
     sibling = place(c_=1 - c)
     after = (grp, (dev + 1) % 32)
-    ks = (1, 3, 2)
+    ks = (2, 1, 3)
     xs = {k: place(x_=flip(x, k)) for k in ks}
     ys = {k: place(y_=flip(y, k)) for k in ks}
     zhs = {k: place(zh_=flip(zh, k)) for k in ks}

time: 74.7 us -> 74 us (level)
  Pallas kernels: 73 us -> 72.2 us
    pallas_call x1, Pallas kernels: 71.3 us -> 70.4 us  [body(): pl.pallas_call(kernel, out_shape=out_shape, in_specs=[hbm] * 11, out_spec...]
where the time goes in v7:
time: 74 us; the launch traced here: 72.8 us
  Pallas kernels  72.2 us (98%)
    pallas_call x1, Pallas kernels, body(): pl.pallas_call(kernel, out_shape=out_shape, in_specs=[hbm] * 11, out_spec...  70.4 us
    pallas_call x1, Pallas kernels, body(): pl.pallas_call(hand_on, out_shape=out_shape, in_specs=[hbm] * 6, out_spec...  1.79 us

profile of v7, /device:TPU:1, one launch (start us, length us, event | category | flops | bytes accessed | tf_op | source)
XLA Modules:
  0.0 72.8 jit_solution(14802608107867931473)
XLA Ops:
  0.6 70.4 %train.1 = (bf16[400,128]{1,0:T(8,128)(2,1)}, f32[1,128]{1,0:T(1,128)}, bf16[400,128]{1,0:T(8,128)(2,1)}, f32[1,128]{1,0:T(1,128)}, f32[65,400]{1,0:T(8,128)}, /*index=5*/f32[1,65]{1,0:T(1,128)}) custom-call(bf16[400,128]{1,0:T(8,128)(2,1)} %bitcast.10, f32[1,128]{1,0:T(1,128)} %bitcast.12, bf16[400,128]{1,0:T(8,128)(2,1)} %bitcast.11, f32[1,128]{1,0:T(1,128)} %bitcast.13, ...), custom_call_target="tpu_custom_call" | custom-call | tf_op jit(solution)/shard_map/train/pallas_call | solution.py:483
  71.1 1.8 %hand_on.1 = (bf16[400,128]{1,0:T(8,128)(2,1)}, f32[1,128]{1,0:T(1,128)}, bf16[400,128]{1,0:T(8,128)(2,1)}, f32[1,128]{1,0:T(1,128)}, f32[65,400]{1,0:T(8,128)}, /*index=5*/f32[1,65]{1,0:T(1,128)}) custom-call(bf16[400,128]{1,0:T(8,128)(2,1)} %get-tuple-element.18.refs_0_, f32[1,128]{1,0:T(1,128)} %get-tuple-element.19.refs_1_, ...), custom_call_target="tpu_custom_call" | custom-call | tf_op jit(solution)/shard_map/hand_on/pallas_call | solution.py:541

commit v8 on v7

--- a/solution.py
+++ b/solution.py
@@ -75,7 +75,7 @@
     lhs_ref, lst_ref, rhs_ref, rst_ref, rel_ref, relst_ref, src_ref, dst_ref, kind_ref, neg_ref, count_ref,
     lhs_out, lst_out, rhs_out, rst_out, rel_out, relst_out,
     times_buf, row_sums, table, left, spare, hot_all, hot_spare, hot_mine, hot_mine_spare, kinds, wide, a_buf, rr_buf, q_buf, m_hi, m_lo, edges,
-    rhs_send, rst_send, rhs_in, rst_in, part, part_left, l_in, l_y, x_in, y_in, x2_in, y2_in, z_out, z_in, low, stage2x, stage2y,
+    rhs_send, rst_send, rhs_in, rst_in, part, part_left, l_in, l_y, x_in, y_in, x2_in, y2_in, z_out, z_in, low, whole, stage2x, stage2y,
     send_sem, recv_sem, in_sem, out_sem,
 ):
     grp, dev = lax.axis_index("grp"), lax.axis_index("dev")
@@ -97,11 +97,6 @@
     ys = {k: place(y_=flip(y, k)) for k in ks}
     zhs = {k: place(zh_=flip(zh, k)) for k in ks}
     zls = {k: place(zl_=flip(zl, k)) for k in ks}
-
-    barrier = pltpu.get_barrier_semaphore()
-    greet = [sibling, *xs.values(), *ys.values(), zhs[1], zhs[3], *zls.values()]
-    for other in greet:
-        pl.semaphore_signal(barrier, inc=1, device_id=other, device_id_type=MESH)
 
     loads = [
         pltpu.make_async_copy(src, dst, in_sem.at[i])
@@ -115,6 +110,11 @@
     ]
     for copy in loads[:2]:
         copy.start()
+    barrier = pltpu.get_barrier_semaphore()
+    greet = [sibling, *xs.values(), *ys.values(), zhs[1], zhs[3], *zls.values()]
+    for other in greet:
+        pl.semaphore_signal(barrier, inc=1, device_id=other, device_id_type=MESH)
+
     started, stores = [], []
 
     def give(src, dst):
@@ -144,15 +144,13 @@
 
     edges[D:WIDE, :] = jnp.zeros((WIDE - D, 4 * SLOTS), BF16)
     wide[...] = jnp.zeros(wide.shape, F32)
-    for copy in loads[:2]:
-        copy.wait()
+    loads[0].wait()
     wide[0:OWN, 0:D] = rel_ref[...]
     table[zh, x, c] = wide[0:ROWS, :].astype(BF16)
     last_row = [wide[ROWS:OWN, LANE * i : LANE * i + LANE] for i in range(4)]
     left[zh, x, c] = jnp.concatenate(
         [fold(wide[0:ROWS, MAIN:WIDE]), *last_row, jnp.zeros((4, LANE), F32)], axis=0
     ).astype(BF16)
-    kinds[c] = jnp.concatenate([kind_ref[0], jnp.zeros((6, SLOTS), I32)], axis=0)
 
     pl.semaphore_wait(barrier, len(greet))
 
@@ -160,6 +158,8 @@
     quarter = table.at[zh, x, c, rows(y), 0:MAIN]
     to_zh = {k: [send(quarter, quarter, zhs[k]), send(mine_left, mine_left, zhs[k])] for k in (1, 3)}
     own_x = [send(mine, mine, xs[k]) for k in ks] + [send(mine_left, mine_left, xs[k]) for k in ks]
+    loads[1].wait()
+    kinds[c] = jnp.concatenate([kind_ref[0], jnp.zeros((6, SLOTS), I32)], axis=0)
     kinds_sib = send(kinds.at[c], kinds.at[c], sibling)
 
     for copy in loads[2:]:
@@ -431,13 +431,14 @@
     zb = [send(low.at[zl], low.at[zl], zls[k]) for k in ks]
     arrived(zb)
     both_z = (low[0].astype(F32) + low[1].astype(F32)) + (low[2].astype(F32) + low[3].astype(F32))
-    own_rows = wide.at[rows(y), 0:MAIN]
-    own_rows[...] = both_z[:, 0:MAIN]
+    own_rows = whole.at[rows(y)]
+    own_rows[...] = both_z[:, 0:MAIN].astype(BF16)
     last = [send(own_rows, own_rows, ys[k]) for k in ks]
     wide[0:ROWS, MAIN:WIDE] = unfold(both_z[0:8, MAIN:WIDE].reshape(1, 8, LANE), 1)[0]
     for i in range(4):
         wide[ROWS:OWN, LANE * i : LANE * i + LANE] = both_z[8 + i : 9 + i, MAIN:WIDE]
     arrived(last)
+    wide[0:ROWS, 0:MAIN] = whole[...].astype(F32)
 
     total = wide[0:OWN, 0:D]
     eye = lax.broadcasted_iota(I32, (OWN, OWN), 0) == lax.broadcasted_iota(I32, (OWN, OWN), 1)
@@ -523,6 +524,7 @@
             pltpu.VMEM((4, 16, WIDE), BF16),
             pltpu.VMEM((3, 16, WIDE), BF16),
             pltpu.VMEM((4, 16, WIDE), BF16),
+            pltpu.VMEM((ROWS, MAIN), BF16),
             pltpu.VMEM((2, 4, 16, MAIN), BF16),
             pltpu.VMEM((2, ROWS, MAIN), BF16),
             pltpu.SemaphoreType.DMA((N_COPIES,)),

time: 74 us -> 73.7 us (level)
  no operation moved by 1% of the time
where the time goes in v8:
time: 73.7 us; the launch traced here: 72.6 us
  Pallas kernels  71.9 us (98%)
    pallas_call x1, Pallas kernels, body(): pl.pallas_call(kernel, out_shape=out_shape, in_specs=[hbm] * 11, out_spec...  70.2 us
    pallas_call x1, Pallas kernels, body(): pl.pallas_call(hand_on, out_shape=out_shape, in_specs=[hbm] * 6, out_spec...  1.79 us

profile of v8, /device:TPU:1, one launch (start us, length us, event | category | flops | bytes accessed | tf_op | source)
XLA Modules:
  0.0 72.6 jit_solution(17979486618974602907)
XLA Ops:
  0.6 70.2 %train.1 = (bf16[400,128]{1,0:T(8,128)(2,1)}, f32[1,128]{1,0:T(1,128)}, bf16[400,128]{1,0:T(8,128)(2,1)}, f32[1,128]{1,0:T(1,128)}, f32[65,400]{1,0:T(8,128)}, /*index=5*/f32[1,65]{1,0:T(1,128)}) custom-call(bf16[400,128]{1,0:T(8,128)(2,1)} %bitcast.10, f32[1,128]{1,0:T(1,128)} %bitcast.12, bf16[400,128]{1,0:T(8,128)(2,1)} %bitcast.11, f32[1,128]{1,0:T(1,128)} %bitcast.13, ...), custom_call_target="tpu_custom_call" | custom-call | tf_op jit(solution)/shard_map/train/pallas_call | solution.py:484
  70.8 1.8 %hand_on.1 = (bf16[400,128]{1,0:T(8,128)(2,1)}, f32[1,128]{1,0:T(1,128)}, bf16[400,128]{1,0:T(8,128)(2,1)}, f32[1,128]{1,0:T(1,128)}, f32[65,400]{1,0:T(8,128)}, /*index=5*/f32[1,65]{1,0:T(1,128)}) custom-call(bf16[400,128]{1,0:T(8,128)(2,1)} %get-tuple-element.18.refs_0_, f32[1,128]{1,0:T(1,128)} %get-tuple-element.19.refs_1_, ...), custom_call_target="tpu_custom_call" | custom-call | tf_op jit(solution)/shard_map/hand_on/pallas_call | solution.py:543
